TPU v7x, 32 devices: a whole 2x2x4 slice. The times are simulated.
32 devices in a mesh: wide: 16 (over z, y, x), narrow: 2 (over core).
Axes of the slice: x: 2, y: 2, z: 4, core: 2. Of those that a mesh axis runs over, the one named last changes fastest.
Arguments:
- kernel: float32 [2048, 64, 128], P(('wide', 'narrow')), may hold values from 0 to 0.015625
- volume: float32 [2048, 64], P(('wide', 'narrow')), may hold values from 0.5 to 4
- velocity: float32 [2048, 3, 64], P(('wide', 'narrow')), may hold values from -6 to 6
- block_brick: int32 [2048, 1], P(('wide', 'narrow')), may hold values from 0 to 15; in each aligned block of 64 rows (0 to 63, 64 to 127, ...) at most 8 rows name the same one
- block_tile: int32 [2048], P(('wide', 'narrow')), may hold values from 0 to 127
- fluid_velocity: float32 [3, 64, 16, 512], P(None, 'wide', 'narrow'), may hold values from -6 to 6
Outputs:
- particle_drag: float32 [2048, 3, 64], P(('wide', 'narrow'))
- pressure: float32 [64, 16, 512], P('wide', 'narrow')
- fluid_next: float32 [3, 64, 16, 512], P(None, 'wide', 'narrow')
Inputs may be any that keep to these rules, and one draw needn't show every extreme that they name: `block_brick`: among the 64 blocks of one device, at most 8 name the same brick, a bound that some block reaches.
All inputs are finite; a program needn't handle non-finite values.
Results may differ from a plain program's by a relative error of at most 0.00007.
Values sent between devices are 32-bit elements; how exact they have to be, the bound alone decides.
A program may use at most 64 MiB of HBM per device.

v0:
```python
import jax
import jax.numpy as jnp
from jax import lax
from jax.sharding import PartitionSpec as P

SWEEPS = 6


highest = lax.Precision.HIGHEST


def with_halo(block, sides, width):
    for axis, dim in sides:
        count = lax.axis_size(axis)
        forward = [(i, i + 1) for i in range(count - 1)]
        backward = [(target, source) for source, target in forward]
        low = lax.ppermute(
            lax.slice_in_dim(block, block.shape[dim] - width, None, axis=dim), axis, forward
        )
        high = lax.ppermute(lax.slice_in_dim(block, 0, width, axis=dim), axis, backward)
        block = jnp.concatenate([low, block, high], axis=dim)
    return block


def neighbours(padded):
    return [
        padded[..., 2:, 1:-1, 1:-1],
        padded[..., :-2, 1:-1, 1:-1],
        padded[..., 1:-1, 2:, 1:-1],
        padded[..., 1:-1, :-2, 1:-1],
        padded[..., 1:-1, 1:-1, 2:],
        padded[..., 1:-1, 1:-1, :-2],
    ]


def pad_third(field):
    return jnp.pad(field, ((0, 0), (0, 0), (0, 0), (1, 1)))


def pressure_sides(pressure):
    ghosted = with_halo(pressure[None], (("wide", 1), ("narrow", 2)), 1)
    return [side[0] for side in neighbours(pad_third(ghosted))]


def local(kernel, volume, velocity, block_brick, block_tile, fluid_velocity):
    n_wide = lax.axis_size("wide")
    blocks = kernel.shape[0]
    cells_tile = kernel.shape[2]
    capacity = max(2, (2 * blocks + n_wide - 1) // n_wide)
    slot_count = n_wide * capacity
    extent = fluid_velocity.shape[1:]
    tile_count = extent[0] * extent[1] * extent[2] // cells_tile
    target = block_brick[:, 0]
    matches = (target[:, None] == jnp.arange(n_wide, dtype=jnp.int32)[None, :]).astype(jnp.int32)
    position = jnp.sum((jnp.cumsum(matches, axis=0) - 1) * matches, axis=1)
    placed = target * capacity + position
    carried = jnp.concatenate([volume[:, None, :], volume[:, None, :] * velocity], axis=1)
    tile_number = block_tile.astype(jnp.float32)
    tile_range = jnp.arange(tile_count, dtype=jnp.float32)
    own_sums = jnp.einsum("bkp,bpc->bkc", carried, kernel, precision=highest)
    own_sums = jnp.concatenate(
        [own_sums, jnp.broadcast_to(tile_number[:, None, None], (blocks, 1, cells_tile))], axis=1
    )
    send_sums = jnp.zeros((slot_count, 5, cells_tile), jnp.float32).at[placed].set(own_sums)
    received = lax.all_to_all(
        send_sums.reshape(n_wide, capacity, 5, cells_tile),
        "wide",
        split_axis=0,
        concat_axis=0,
        tiled=True,
    )
    received = received.reshape(slot_count, 5, cells_tile)
    slot_sums = received[:, :4]
    slot_tiles = received[:, 4, 0]
    selector = (slot_tiles[:, None] == tile_range[None, :]).astype(jnp.float32)
    spread = jnp.einsum("st,skc->ktc", selector, slot_sums, precision=highest).reshape(
        (4,) + extent
    )
    solid_share = spread[0]
    momentum = spread[1:]
    growth = (1.0 + solid_share) ** 2
    provisional = (fluid_velocity + growth * momentum) / (1.0 + growth * solid_share)
    void_share = 1.0 / (1.0 + solid_share)
    stacked = jnp.concatenate([void_share * provisional, void_share[None]], axis=0)
    ghosted = with_halo(stacked, (("wide", 1), ("narrow", 2)), 1)
    sides = neighbours(pad_third(ghosted))
    source = -0.5 * (
        sides[0][0] - sides[1][0] + sides[2][1] - sides[3][1] + sides[4][2] - sides[5][2]
    )
    weights = [0.5 * (void_share + side[3]) for side in sides]
    diagonal = weights[0] + weights[1] + weights[2] + weights[3] + weights[4] + weights[5]
    pressure = source / diagonal
    for sweep_index in range(SWEEPS - 1):
        beside_all = pressure_sides(pressure)
        total = source
        for which in range(6):
            total = total + weights[which] * beside_all[which]
        pressure = total / diagonal
    beside_all = pressure_sides(pressure)
    fluid_next = provisional - 0.5 * jnp.stack(
        [
            beside_all[0] - beside_all[1],
            beside_all[2] - beside_all[3],
            beside_all[4] - beside_all[5],
        ]
    )
    coupled = jnp.concatenate([growth * fluid_next, growth[None]], axis=0).reshape(
        4, tile_count, cells_tile
    )
    picked = jnp.einsum("st,ktc->skc", selector, coupled, precision=highest)
    returned = lax.all_to_all(
        picked.reshape(n_wide, capacity, 4, cells_tile),
        "wide",
        split_axis=0,
        concat_axis=0,
        tiled=True,
    )
    block_fields = returned.reshape(slot_count, 4, cells_tile)[placed]
    sampled = jnp.einsum("bkc,bpc->bkp", block_fields, kernel, precision=highest)
    particle_drag = volume[:, None, :] * sampled[:, :3] - carried[:, 1:] * sampled[:, 3:4]
    return (particle_drag, pressure, fluid_next)


def solution(mesh):
    return jax.shard_map(
        local,
        mesh=mesh,
        in_specs=(
            P(("wide", "narrow"), None, None),
            P(("wide", "narrow"), None),
            P(("wide", "narrow"), None, None),
            P(("wide", "narrow"), None),
            P(("wide", "narrow")),
            P(None, "wide", "narrow", None),
        ),
        out_specs=(
            P(("wide", "narrow"), None, None),
            P("wide", "narrow", None),
            P(None, "wide", "narrow", None),
        ),
        check_vma=False,
    )
```

profile of v0, /device:TPU:0, one launch (start us, length us, event | category | flops | bytes accessed | tf_op | source)
XLA Modules:
  0.0 169.9 jit_solution(3262792454113317037)
XLA Ops:
  0.6 0.9 fusion.78
  1.6 0.8 select_reduce_fusion
  2.5 0.7 fusion.79
  3.1 0.7 convert_element_type.17
  3.8 1.0 copy_multiply_fusion
  4.8 2.5 %fusion.7 = f32[64,4,128]{2,1,0:T(4,128)S(1)} fusion(f32[64,64,128]{2,1,0:T(8,128)S(1)} %copy-done, f32[64,3,64]{2,1,0:T(4,128)S(1)} %copy_multiply_fusion, f32[64,1,64]{2,1,0:T(1,128)} %bitcast.112), kind=kOutput, calls=%fused_computation.50 | convolution fusion | flops 25182208 | bytes 2293760 | tf_op jit(solution)/shard_map/bkp,bpc->bkc/dot_general | solution.py:60
  7.6 2.4 %scatter_fusion = f32[128,5,128]{2,1,0:T(8,128)S(1)} fusion(f32[128,5,128]{2,1,0:T(8,128)S(1)} %broadcast_in_dim.6, s32[64]{0:T(128)S(1)} %fusion.79, f32[64,5,128]{2,1,0:T(8,128)S(1)} %pad_maximum_fusion), kind=kCustom, calls=%fused_computation.1 | custom fusion | bytes 491776 | tf_op jit(solution)/shard_map/scatter | solution.py:64
  10.1 19.6 %all_to_all.10 = f32[16,8,5,128]{3,1,2,0:T(8,128)S(1)} all-to-all(f32[16,8,5,128]{3,1,2,0:T(8,128)S(1)} %copy.34), channel_id=1, replica_groups=mesh['wide'=16,'narrow'=2] {'wide'}, dimensions={0} | all-to-all | bytes 655360 | tf_op jit(solution)/shard_map/all_to_all | solution.py:65
  32.0 1.3 collective-permute-start
  33.3 4.5 %collective-permute-start.1 = (f32[4,1,8,512]{3,2,1,0:T(8,128)S(1)}, f32[4,1,8,512]{3,2,1,0:T(8,128)S(1)}, u32[]{:S(2)}, u32[]{:S(2)}) collective-permute-start(f32[4,1,8,512]{3,2,1,0:T(8,128)S(1)} %get-tuple-element.31), channel_id=1, source_target_pairs={{0,2},{2,4},{4,6},{6,8},{8,10},{10,12},{12,14},{14,16},{16,18},{18... | collective-permute-start | bytes 196616 | tf_op jit(solution)/shard_map/ppermute | solution.py:17
  38.3 1.4 collective-permute-done.1
  39.8 1.3 collective-permute-start.2
  41.1 3.0 %collective-permute-start.3 = (f32[4,6,1,512]{3,2,1,0:T(1,128)S(1)}, f32[4,6,1,512]{3,2,1,0:T(1,128)S(1)}, u32[]{:S(2)}, u32[]{:S(2)}) collective-permute-start(f32[4,6,1,512]{3,2,1,0:T(1,128)S(1)} %get-tuple-element.29), channel_id=1, source_target_pairs={{0,1},{2,3},{4,5},{6,7},{8,9},{10,11},{12,13},{14,15},{16,17},{18,... | collective-permute-start | bytes 147464 | tf_op jit(solution)/shard_map/ppermute | solution.py:17
  44.1 0.9 collective-permute-done.3
  45.6 0.8 fusion.71
  46.4 1.3 collective-permute-start.4
  47.7 4.9 %collective-permute-start.5 = (f32[1,1,8,512]{3,2,1,0:T(8,128)S(1)}, f32[1,1,8,512]{3,2,1,0:T(8,128)S(1)}, u32[]{:S(2)}, u32[]{:S(2)}) collective-permute-start(f32[1,1,8,512]{3,2,1,0:T(8,128)S(1)} %get-tuple-element.60), channel_id=1, source_target_pairs={{0,2},{2,4},{4,6},{6,8},{8,10},{10,12},{12,14},{14,16},{16,18},{18... | collective-permute-start | bytes 49160 | tf_op jit(solution)/shard_map/ppermute | solution.py:17
  52.6 1.4 collective-permute-done.5
  54.0 1.3 collective-permute-start.6
  55.3 3.0 %collective-permute-start.7 = (f32[1,6,1,512]{3,2,1,0:T(1,128)S(1)}, f32[1,6,1,512]{3,2,1,0:T(1,128)S(1)}, u32[]{:S(2)}, u32[]{:S(2)}) collective-permute-start(f32[1,6,1,512]{3,2,1,0:T(1,128)S(1)} %get-tuple-element.48), channel_id=1, source_target_pairs={{0,1},{2,3},{4,5},{6,7},{8,9},{10,11},{12,13},{14,15},{16,17},{18,... | collective-permute-start | bytes 36872 | tf_op jit(solution)/shard_map/ppermute | solution.py:17
  58.4 0.8 collective-permute-done.7
  59.5 1.3 collective-permute-start.8
  60.8 5.4 %collective-permute-start.9 = (f32[1,1,8,512]{3,2,1,0:T(8,128)S(1)}, f32[1,1,8,512]{3,2,1,0:T(8,128)S(1)}, u32[]{:S(2)}, u32[]{:S(2)}) collective-permute-start(f32[1,1,8,512]{3,2,1,0:T(8,128)S(1)} %get-tuple-element.58), channel_id=1, source_target_pairs={{0,2},{2,4},{4,6},{6,8},{8,10},{10,12},{12,14},{14,16},{16,18},{18... | collective-permute-start | bytes 49160 | tf_op jit(solution)/shard_map/ppermute | solution.py:17
  66.2 1.4 collective-permute-done.9
  67.7 1.3 collective-permute-start.10
  69.0 3.0 %collective-permute-start.11 = (f32[1,6,1,512]{3,2,1,0:T(1,128)S(1)}, f32[1,6,1,512]{3,2,1,0:T(1,128)S(1)}, u32[]{:S(2)}, u32[]{:S(2)}) collective-permute-start(f32[1,6,1,512]{3,2,1,0:T(1,128)S(1)} %get-tuple-element.46), channel_id=1, source_target_pairs={{0,1},{2,3},{4,5},{6,7},{8,9},{10,11},{12,13},{14,15},{16,17},{18,... | collective-permute-start | bytes 36872 | tf_op jit(solution)/shard_map/ppermute | solution.py:17
  72.0 0.8 collective-permute-done.11
  73.1 1.3 collective-permute-start.12
  74.4 5.7 %collective-permute-start.13 = (f32[1,1,8,512]{3,2,1,0:T(8,128)S(1)}, f32[1,1,8,512]{3,2,1,0:T(8,128)S(1)}, u32[]{:S(2)}, u32[]{:S(2)}) collective-permute-start(f32[1,1,8,512]{3,2,1,0:T(8,128)S(1)} %get-tuple-element.56), channel_id=1, source_target_pairs={{0,2},{2,4},{4,6},{6,8},{8,10},{10,12},{12,14},{14,16},{16,18},{18... | collective-permute-start | bytes 49160 | tf_op jit(solution)/shard_map/ppermute | solution.py:17
  80.2 1.4 collective-permute-done.13
  81.6 1.3 collective-permute-start.14
  82.9 3.0 %collective-permute-start.15 = (f32[1,6,1,512]{3,2,1,0:T(1,128)S(1)}, f32[1,6,1,512]{3,2,1,0:T(1,128)S(1)}, u32[]{:S(2)}, u32[]{:S(2)}) collective-permute-start(f32[1,6,1,512]{3,2,1,0:T(1,128)S(1)} %get-tuple-element.44), channel_id=1, source_target_pairs={{0,1},{2,3},{4,5},{6,7},{8,9},{10,11},{12,13},{14,15},{16,17},{18,... | collective-permute-start | bytes 36872 | tf_op jit(solution)/shard_map/ppermute | solution.py:17
  86.0 0.8 collective-permute-done.15
  87.1 1.3 collective-permute-start.16
  88.4 5.7 %collective-permute-start.17 = (f32[1,1,8,512]{3,2,1,0:T(8,128)S(1)}, f32[1,1,8,512]{3,2,1,0:T(8,128)S(1)}, u32[]{:S(2)}, u32[]{:S(2)}) collective-permute-start(f32[1,1,8,512]{3,2,1,0:T(8,128)S(1)} %get-tuple-element.54), channel_id=1, source_target_pairs={{0,2},{2,4},{4,6},{6,8},{8,10},{10,12},{12,14},{14,16},{16,18},{18... | collective-permute-start | bytes 49160 | tf_op jit(solution)/shard_map/ppermute | solution.py:17
  94.1 1.4 collective-permute-done.17
  95.6 1.3 collective-permute-start.18
  96.9 3.0 %collective-permute-start.19 = (f32[1,6,1,512]{3,2,1,0:T(1,128)S(1)}, f32[1,6,1,512]{3,2,1,0:T(1,128)S(1)}, u32[]{:S(2)}, u32[]{:S(2)}) collective-permute-start(f32[1,6,1,512]{3,2,1,0:T(1,128)S(1)} %get-tuple-element.42), channel_id=1, source_target_pairs={{0,1},{2,3},{4,5},{6,7},{8,9},{10,11},{12,13},{14,15},{16,17},{18,... | collective-permute-start | bytes 36872 | tf_op jit(solution)/shard_map/ppermute | solution.py:17
  99.9 0.8 collective-permute-done.19
  101.0 1.3 collective-permute-start.20
  102.3 5.7 %collective-permute-start.21 = (f32[1,1,8,512]{3,2,1,0:T(8,128)S(1)}, f32[1,1,8,512]{3,2,1,0:T(8,128)S(1)}, u32[]{:S(2)}, u32[]{:S(2)}) collective-permute-start(f32[1,1,8,512]{3,2,1,0:T(8,128)S(1)} %get-tuple-element.52), channel_id=1, source_target_pairs={{0,2},{2,4},{4,6},{6,8},{8,10},{10,12},{12,14},{14,16},{16,18},{18... | collective-permute-start | bytes 49160 | tf_op jit(solution)/shard_map/ppermute | solution.py:17
  108.1 1.4 collective-permute-done.21
  109.5 1.3 collective-permute-start.22
  110.8 3.0 %collective-permute-start.23 = (f32[1,6,1,512]{3,2,1,0:T(1,128)S(1)}, f32[1,6,1,512]{3,2,1,0:T(1,128)S(1)}, u32[]{:S(2)}, u32[]{:S(2)}) collective-permute-start(f32[1,6,1,512]{3,2,1,0:T(1,128)S(1)} %get-tuple-element.40), channel_id=1, source_target_pairs={{0,1},{2,3},{4,5},{6,7},{8,9},{10,11},{12,13},{14,15},{16,17},{18,... | collective-permute-start | bytes 36872 | tf_op jit(solution)/shard_map/ppermute | solution.py:17
  113.9 0.8 collective-permute-done.23
  115.6 5.1 %collective-permute-start.25 = (f32[1,1,8,512]{3,2,1,0:T(8,128)S(1)}, f32[1,1,8,512]{3,2,1,0:T(8,128)S(1)}, u32[]{:S(2)}, u32[]{:S(2)}) collective-permute-start(f32[1,1,8,512]{3,2,1,0:T(8,128)S(1)} %get-tuple-element.50), channel_id=1, source_target_pairs={{0,2},{2,4},{4,6},{6,8},{8,10},{10,12},{12,14},{14,16},{16,18},{18... | collective-permute-start | bytes 49160 | tf_op jit(solution)/shard_map/ppermute | solution.py:17
  120.7 1.3 collective-permute-start.24
  122.1 5.4 %collective-permute-done.24 = f32[1,1,8,512]{3,2,1,0:T(8,128)S(1)} collective-permute-done((f32[1,1,8,512]{3,2,1,0:T(8,128)S(1)}, f32[1,1,8,512]{3,2,1,0:T(8,128)S(1)}, u32[]{:S(2)}, u32[]{:S(2)}) %collective-permute-start.24) | collective-permute-done | bytes 16416 | tf_op jit(solution)/shard_map/ppermute | solution.py:20
  128.1 1.9 %collective-permute-start.27 = (f32[1,6,1,512]{3,2,1,0:T(1,128)}, f32[1,6,1,512]{3,2,1,0:T(1,128)}, u32[]{:S(2)}, u32[]{:S(2)}) collective-permute-start(f32[1,6,1,512]{3,2,1,0:T(1,128)} %get-tuple-element.38), channel_id=1, source_target_pairs={{0,1},{2,3},{4,5},{6,7},{8,9},{10,11},{12,13},{14,15},{16,17},{18,... | collective-permute-start | bytes 36872 | tf_op jit(solution)/shard_map/ppermute | solution.py:17
  130.0 1.3 collective-permute-start.26
  131.3 1.3 eq.43
  132.6 1.6 copy.40
  134.2 1.0 select_maximum_fusion.5
  135.2 0.8 fusion.12
  136.0 1.8 %broadcast_multiply_fusion.1 = (f32[3,4,8,512]{3,2,1,0:T(8,128)}, f32[3,4,8,512]{3,2,1,0:T(8,128)}) fusion(f32[4,8,512]{2,1,0:T(8,128)} %copy-done.3, f32[1,4,8,512]{3,2,1,0:T(8,128)S(1)} %get-tuple-element.65, f32[1,4,8,512]{3,2,1,0:T(8,128)S(1)} %get-tuple-element.37, f32[1,4,8,512]{3,2,1,0:T(8,128)S(1)} %get-tuple-element.36, ...), kind=kLoop, calls=%fused_computation.56 | loop fusion | flops 393216 | bytes 1114112 | tf_op jit(solution)/shard_map/mul | solution.py:107
  137.8 0.9 concatenate.190
  138.8 1.9 %fusion.1 = f32[16,8,4,128]{3,1,2,0:T(8,128)} fusion(f32[1,128,128]{2,1,0:T(8,128)} %copy.40, f32[3,128,128]{2,1,0:T(8,128)S(1)} %concatenate.190, f32[16,8]{1,0:T(8,128)} %eq.43), kind=kOutput, calls=%fused_computation.16 | convolution fusion | flops 100745216 | bytes 524800 | tf_op jit(solution)/shard_map/st,ktc->skc/dot_general | solution.py:110
  140.7 13.0 %all-to-all-start.1 = ((f32[16,8,4,128]{3,1,2,0:T(8,128)}), f32[16,8,4,128]{3,1,2,0:T(8,128)}, u32[]{:S(2)}, u32[]{:S(2)}) async-start(f32[16,8,4,128]{3,1,2,0:T(8,128)} %fusion.1), calls=%async_computation.1 | async-start | bytes 524288 | tf_op jit(solution)/shard_map/all_to_all | solution.py:111
  153.6 0.7 pad_clamp_fusion
  154.3 1.9 %fusion.59 = f32[4,8,512]{2,1,0:T(8,128)} fusion(f32[1,4,8,512]{3,2,1,0:T(8,128)S(1)} %get-tuple-element.20, f32[1,4,8,512]{3,2,1,0:T(8,128)} %get-tuple-element.26, f32[1,4,8,512]{3,2,1,0:T(8,128)} %get-tuple-element.24, f32[1,4,8,512]{3,2,1,0:T(8,128)} %get-tuple-element.19, f32[1,4,8,512]{3,2,1,0:T(8,128)} %get-tuple-element.22, ...), kind=kLoop, calls=%fused_computation.183 | loop fusion | flops 655360 | bytes 843776 | tf_op jit(solution)/shard_map/div | solution.py:98
  156.2 7.7 %all-to-all-done.1 = f32[16,8,4,128]{3,1,2,0:T(8,128)} async-done(((f32[16,8,4,128]{3,1,2,0:T(8,128)}), f32[16,8,4,128]{3,1,2,0:T(8,128)}, u32[]{:S(2)}, u32[]{:S(2)}) %all-to-all-start.1) | async-done | bytes 262176 | tf_op jit(solution)/shard_map/all_to_all | solution.py:111
  163.9 1.0 copy.55
  165.0 0.7 gather_fusion
  165.7 3.4 %fusion.90 = f32[64,4,64]{2,1,0:T(4,128)S(1)} fusion(f32[64,4,128]{2,1,0:T(4,128)S(1)} %gather_fusion, f32[64,64,128]{2,1,0:T(8,128)S(1)} %copy-done), kind=kOutput, calls=%fused_computation.263 | convolution fusion | flops 25165824 | bytes 2293760 | tf_op jit(solution)/shard_map/bkc,bpc->bkp/dot_general | solution.py:119
  (92 shorter events, 7.7 us)
Async XLA Ops:
  0.6 4.1 %copy-start = (f32[64,64,128]{2,1,0:T(8,128)S(1)}, f32[64,64,128]{2,1,0:T(8,128)}, u32[]{:S(2)}) copy-start(f32[64,64,128]{2,1,0:T(8,128)} %param.6) | copy-start | bytes 6291460
  3.1 6.9 %copy-start.14 = (s32[64]{0:T(128)}, s32[64]{0:T(128)S(1)}, u32[]{:S(2)}) copy-start(s32[64]{0:T(128)S(1)} %fusion.79) | copy-start | bytes 772
  10.1 21.8 %copy-start.2 = (f32[3,4,8,512]{3,2,1,0:T(8,128)S(1)}, f32[3,4,8,512]{3,2,1,0:T(8,128)}, u32[]{:S(2)}) copy-start(f32[3,4,8,512]{3,2,1,0:T(8,128)} %param.11) | copy-start | bytes 589828
  29.8 10.0 %copy-start.13 = (f32[128]{0:T(128)}, f32[128]{0:T(128)S(1)}, u32[]{:S(2)}) copy-start(f32[128]{0:T(128)S(1)} %slice_reduce_fusion) | copy-start | bytes 1540
  31.0 0.6 copy-start.4
  31.0 14.6 %copy-start.3 = (f32[4,8,512]{2,1,0:T(8,128)}, f32[4,8,512]{2,1,0:T(8,128)S(1)}, u32[]{:S(2)}) copy-start(f32[4,8,512]{2,1,0:T(8,128)S(1)} %get-tuple-element.64) | copy-start | bytes 196612
  32.0 6.3 %collective-permute-start = (f32[4,1,8,512]{3,2,1,0:T(8,128)S(1)}, f32[4,1,8,512]{3,2,1,0:T(8,128)S(1)}, u32[]{:S(2)}, u32[]{:S(2)}) collective-permute-start(f32[4,1,8,512]{3,2,1,0:T(8,128)S(1)} %get-tuple-element.32), channel_id=1, source_target_pairs={{2,0},{4,2},{6,4},{8,6},{10,8},{12,10},{14,12},{16,14},{18,16},{20... | collective-permute-start | bytes 196616 | tf_op jit(solution)/shard_map/ppermute | solution.py:20
  33.3 6.4 %collective-permute-start.1 = (f32[4,1,8,512]{3,2,1,0:T(8,128)S(1)}, f32[4,1,8,512]{3,2,1,0:T(8,128)S(1)}, u32[]{:S(2)}, u32[]{:S(2)}) collective-permute-start(f32[4,1,8,512]{3,2,1,0:T(8,128)S(1)} %get-tuple-element.31), channel_id=1, source_target_pairs={{0,2},{2,4},{4,6},{6,8},{8,10},{10,12},{12,14},{14,16},{16,18},{18... | collective-permute-start | bytes 196616 | tf_op jit(solution)/shard_map/ppermute | solution.py:17
  39.8 4.3 %collective-permute-start.2 = (f32[4,6,1,512]{3,2,1,0:T(1,128)S(1)}, f32[4,6,1,512]{3,2,1,0:T(1,128)S(1)}, u32[]{:S(2)}, u32[]{:S(2)}) collective-permute-start(f32[4,6,1,512]{3,2,1,0:T(1,128)S(1)} %get-tuple-element.30), channel_id=1, source_target_pairs={{1,0},{3,2},{5,4},{7,6},{9,8},{11,10},{13,12},{15,14},{17,16},{19,... | collective-permute-start | bytes 147464 | tf_op jit(solution)/shard_map/ppermute | solution.py:20
  41.1 3.9 %collective-permute-start.3 = (f32[4,6,1,512]{3,2,1,0:T(1,128)S(1)}, f32[4,6,1,512]{3,2,1,0:T(1,128)S(1)}, u32[]{:S(2)}, u32[]{:S(2)}) collective-permute-start(f32[4,6,1,512]{3,2,1,0:T(1,128)S(1)} %get-tuple-element.29), channel_id=1, source_target_pairs={{0,1},{2,3},{4,5},{6,7},{8,9},{10,11},{12,13},{14,15},{16,17},{18,... | collective-permute-start | bytes 147464 | tf_op jit(solution)/shard_map/ppermute | solution.py:17
  46.4 6.2 %collective-permute-start.4 = (f32[1,1,8,512]{3,2,1,0:T(8,128)S(1)}, f32[1,1,8,512]{3,2,1,0:T(8,128)S(1)}, u32[]{:S(2)}, u32[]{:S(2)}) collective-permute-start(f32[1,1,8,512]{3,2,1,0:T(8,128)S(1)} %get-tuple-element.61), channel_id=1, source_target_pairs={{2,0},{4,2},{6,4},{8,6},{10,8},{12,10},{14,12},{16,14},{18,16},{20... | collective-permute-start | bytes 49160 | tf_op jit(solution)/shard_map/ppermute | solution.py:20
  47.7 6.3 %collective-permute-start.5 = (f32[1,1,8,512]{3,2,1,0:T(8,128)S(1)}, f32[1,1,8,512]{3,2,1,0:T(8,128)S(1)}, u32[]{:S(2)}, u32[]{:S(2)}) collective-permute-start(f32[1,1,8,512]{3,2,1,0:T(8,128)S(1)} %get-tuple-element.60), channel_id=1, source_target_pairs={{0,2},{2,4},{4,6},{6,8},{8,10},{10,12},{12,14},{14,16},{16,18},{18... | collective-permute-start | bytes 49160 | tf_op jit(solution)/shard_map/ppermute | solution.py:17
  54.0 4.3 %collective-permute-start.6 = (f32[1,6,1,512]{3,2,1,0:T(1,128)S(1)}, f32[1,6,1,512]{3,2,1,0:T(1,128)S(1)}, u32[]{:S(2)}, u32[]{:S(2)}) collective-permute-start(f32[1,6,1,512]{3,2,1,0:T(1,128)S(1)} %get-tuple-element.49), channel_id=1, source_target_pairs={{1,0},{3,2},{5,4},{7,6},{9,8},{11,10},{13,12},{15,14},{17,16},{19,... | collective-permute-start | bytes 36872 | tf_op jit(solution)/shard_map/ppermute | solution.py:20
  55.3 3.9 %collective-permute-start.7 = (f32[1,6,1,512]{3,2,1,0:T(1,128)S(1)}, f32[1,6,1,512]{3,2,1,0:T(1,128)S(1)}, u32[]{:S(2)}, u32[]{:S(2)}) collective-permute-start(f32[1,6,1,512]{3,2,1,0:T(1,128)S(1)} %get-tuple-element.48), channel_id=1, source_target_pairs={{0,1},{2,3},{4,5},{6,7},{8,9},{10,11},{12,13},{14,15},{16,17},{18,... | collective-permute-start | bytes 36872 | tf_op jit(solution)/shard_map/ppermute | solution.py:17
  59.5 6.8 %collective-permute-start.8 = (f32[1,1,8,512]{3,2,1,0:T(8,128)S(1)}, f32[1,1,8,512]{3,2,1,0:T(8,128)S(1)}, u32[]{:S(2)}, u32[]{:S(2)}) collective-permute-start(f32[1,1,8,512]{3,2,1,0:T(8,128)S(1)} %get-tuple-element.59), channel_id=1, source_target_pairs={{2,0},{4,2},{6,4},{8,6},{10,8},{12,10},{14,12},{16,14},{18,16},{20... | collective-permute-start | bytes 49160 | tf_op jit(solution)/shard_map/ppermute | solution.py:20
  60.8 6.9 %collective-permute-start.9 = (f32[1,1,8,512]{3,2,1,0:T(8,128)S(1)}, f32[1,1,8,512]{3,2,1,0:T(8,128)S(1)}, u32[]{:S(2)}, u32[]{:S(2)}) collective-permute-start(f32[1,1,8,512]{3,2,1,0:T(8,128)S(1)} %get-tuple-element.58), channel_id=1, source_target_pairs={{0,2},{2,4},{4,6},{6,8},{8,10},{10,12},{12,14},{14,16},{16,18},{18... | collective-permute-start | bytes 49160 | tf_op jit(solution)/shard_map/ppermute | solution.py:17
  67.7 4.3 %collective-permute-start.10 = (f32[1,6,1,512]{3,2,1,0:T(1,128)S(1)}, f32[1,6,1,512]{3,2,1,0:T(1,128)S(1)}, u32[]{:S(2)}, u32[]{:S(2)}) collective-permute-start(f32[1,6,1,512]{3,2,1,0:T(1,128)S(1)} %get-tuple-element.47), channel_id=1, source_target_pairs={{1,0},{3,2},{5,4},{7,6},{9,8},{11,10},{13,12},{15,14},{17,16},{19,... | collective-permute-start | bytes 36872 | tf_op jit(solution)/shard_map/ppermute | solution.py:20
  69.0 3.9 %collective-permute-start.11 = (f32[1,6,1,512]{3,2,1,0:T(1,128)S(1)}, f32[1,6,1,512]{3,2,1,0:T(1,128)S(1)}, u32[]{:S(2)}, u32[]{:S(2)}) collective-permute-start(f32[1,6,1,512]{3,2,1,0:T(1,128)S(1)} %get-tuple-element.46), channel_id=1, source_target_pairs={{0,1},{2,3},{4,5},{6,7},{8,9},{10,11},{12,13},{14,15},{16,17},{18,... | collective-permute-start | bytes 36872 | tf_op jit(solution)/shard_map/ppermute | solution.py:17
  73.1 7.0 %collective-permute-start.12 = (f32[1,1,8,512]{3,2,1,0:T(8,128)S(1)}, f32[1,1,8,512]{3,2,1,0:T(8,128)S(1)}, u32[]{:S(2)}, u32[]{:S(2)}) collective-permute-start(f32[1,1,8,512]{3,2,1,0:T(8,128)S(1)} %get-tuple-element.57), channel_id=1, source_target_pairs={{2,0},{4,2},{6,4},{8,6},{10,8},{12,10},{14,12},{16,14},{18,16},{20... | collective-permute-start | bytes 49160 | tf_op jit(solution)/shard_map/ppermute | solution.py:20
  74.4 7.2 %collective-permute-start.13 = (f32[1,1,8,512]{3,2,1,0:T(8,128)S(1)}, f32[1,1,8,512]{3,2,1,0:T(8,128)S(1)}, u32[]{:S(2)}, u32[]{:S(2)}) collective-permute-start(f32[1,1,8,512]{3,2,1,0:T(8,128)S(1)} %get-tuple-element.56), channel_id=1, source_target_pairs={{0,2},{2,4},{4,6},{6,8},{8,10},{10,12},{12,14},{14,16},{16,18},{18... | collective-permute-start | bytes 49160 | tf_op jit(solution)/shard_map/ppermute | solution.py:17
  81.6 4.3 %collective-permute-start.14 = (f32[1,6,1,512]{3,2,1,0:T(1,128)S(1)}, f32[1,6,1,512]{3,2,1,0:T(1,128)S(1)}, u32[]{:S(2)}, u32[]{:S(2)}) collective-permute-start(f32[1,6,1,512]{3,2,1,0:T(1,128)S(1)} %get-tuple-element.45), channel_id=1, source_target_pairs={{1,0},{3,2},{5,4},{7,6},{9,8},{11,10},{13,12},{15,14},{17,16},{19,... | collective-permute-start | bytes 36872 | tf_op jit(solution)/shard_map/ppermute | solution.py:20
  82.9 3.9 %collective-permute-start.15 = (f32[1,6,1,512]{3,2,1,0:T(1,128)S(1)}, f32[1,6,1,512]{3,2,1,0:T(1,128)S(1)}, u32[]{:S(2)}, u32[]{:S(2)}) collective-permute-start(f32[1,6,1,512]{3,2,1,0:T(1,128)S(1)} %get-tuple-element.44), channel_id=1, source_target_pairs={{0,1},{2,3},{4,5},{6,7},{8,9},{10,11},{12,13},{14,15},{16,17},{18,... | collective-permute-start | bytes 36872 | tf_op jit(solution)/shard_map/ppermute | solution.py:17
  87.1 7.0 %collective-permute-start.16 = (f32[1,1,8,512]{3,2,1,0:T(8,128)S(1)}, f32[1,1,8,512]{3,2,1,0:T(8,128)S(1)}, u32[]{:S(2)}, u32[]{:S(2)}) collective-permute-start(f32[1,1,8,512]{3,2,1,0:T(8,128)S(1)} %get-tuple-element.55), channel_id=1, source_target_pairs={{2,0},{4,2},{6,4},{8,6},{10,8},{12,10},{14,12},{16,14},{18,16},{20... | collective-permute-start | bytes 49160 | tf_op jit(solution)/shard_map/ppermute | solution.py:20
  88.4 7.2 %collective-permute-start.17 = (f32[1,1,8,512]{3,2,1,0:T(8,128)S(1)}, f32[1,1,8,512]{3,2,1,0:T(8,128)S(1)}, u32[]{:S(2)}, u32[]{:S(2)}) collective-permute-start(f32[1,1,8,512]{3,2,1,0:T(8,128)S(1)} %get-tuple-element.54), channel_id=1, source_target_pairs={{0,2},{2,4},{4,6},{6,8},{8,10},{10,12},{12,14},{14,16},{16,18},{18... | collective-permute-start | bytes 49160 | tf_op jit(solution)/shard_map/ppermute | solution.py:17
  95.6 4.3 %collective-permute-start.18 = (f32[1,6,1,512]{3,2,1,0:T(1,128)S(1)}, f32[1,6,1,512]{3,2,1,0:T(1,128)S(1)}, u32[]{:S(2)}, u32[]{:S(2)}) collective-permute-start(f32[1,6,1,512]{3,2,1,0:T(1,128)S(1)} %get-tuple-element.43), channel_id=1, source_target_pairs={{1,0},{3,2},{5,4},{7,6},{9,8},{11,10},{13,12},{15,14},{17,16},{19,... | collective-permute-start | bytes 36872 | tf_op jit(solution)/shard_map/ppermute | solution.py:20
  96.9 3.9 %collective-permute-start.19 = (f32[1,6,1,512]{3,2,1,0:T(1,128)S(1)}, f32[1,6,1,512]{3,2,1,0:T(1,128)S(1)}, u32[]{:S(2)}, u32[]{:S(2)}) collective-permute-start(f32[1,6,1,512]{3,2,1,0:T(1,128)S(1)} %get-tuple-element.42), channel_id=1, source_target_pairs={{0,1},{2,3},{4,5},{6,7},{8,9},{10,11},{12,13},{14,15},{16,17},{18,... | collective-permute-start | bytes 36872 | tf_op jit(solution)/shard_map/ppermute | solution.py:17
  101.0 7.0 %collective-permute-start.20 = (f32[1,1,8,512]{3,2,1,0:T(8,128)S(1)}, f32[1,1,8,512]{3,2,1,0:T(8,128)S(1)}, u32[]{:S(2)}, u32[]{:S(2)}) collective-permute-start(f32[1,1,8,512]{3,2,1,0:T(8,128)S(1)} %get-tuple-element.53), channel_id=1, source_target_pairs={{2,0},{4,2},{6,4},{8,6},{10,8},{12,10},{14,12},{16,14},{18,16},{20... | collective-permute-start | bytes 49160 | tf_op jit(solution)/shard_map/ppermute | solution.py:20
  102.3 7.2 %collective-permute-start.21 = (f32[1,1,8,512]{3,2,1,0:T(8,128)S(1)}, f32[1,1,8,512]{3,2,1,0:T(8,128)S(1)}, u32[]{:S(2)}, u32[]{:S(2)}) collective-permute-start(f32[1,1,8,512]{3,2,1,0:T(8,128)S(1)} %get-tuple-element.52), channel_id=1, source_target_pairs={{0,2},{2,4},{4,6},{6,8},{8,10},{10,12},{12,14},{14,16},{16,18},{18... | collective-permute-start | bytes 49160 | tf_op jit(solution)/shard_map/ppermute | solution.py:17
  109.5 6.1 %copy-start.8 = (f32[1,1,8,512]{3,2,1,0:T(8,128)}, f32[1,1,8,512]{3,2,1,0:T(8,128)S(1)}, u32[]{:S(2)}) copy-start(f32[1,1,8,512]{3,2,1,0:T(8,128)S(1)} %collective-permute-done.21) | copy-start | bytes 49156
  109.5 4.3 %collective-permute-start.22 = (f32[1,6,1,512]{3,2,1,0:T(1,128)S(1)}, f32[1,6,1,512]{3,2,1,0:T(1,128)S(1)}, u32[]{:S(2)}, u32[]{:S(2)}) collective-permute-start(f32[1,6,1,512]{3,2,1,0:T(1,128)S(1)} %get-tuple-element.41), channel_id=1, source_target_pairs={{1,0},{3,2},{5,4},{7,6},{9,8},{11,10},{13,12},{15,14},{17,16},{19,... | collective-permute-start | bytes 36872 | tf_op jit(solution)/shard_map/ppermute | solution.py:20
  110.8 3.9 %collective-permute-start.23 = (f32[1,6,1,512]{3,2,1,0:T(1,128)S(1)}, f32[1,6,1,512]{3,2,1,0:T(1,128)S(1)}, u32[]{:S(2)}, u32[]{:S(2)}) collective-permute-start(f32[1,6,1,512]{3,2,1,0:T(1,128)S(1)} %get-tuple-element.40), channel_id=1, source_target_pairs={{0,1},{2,3},{4,5},{6,7},{8,9},{10,11},{12,13},{14,15},{16,17},{18,... | collective-permute-start | bytes 36872 | tf_op jit(solution)/shard_map/ppermute | solution.py:17
  113.9 14.3 %copy-start.11 = (f32[1,6,1,512]{3,2,1,0:T(1,128)}, f32[1,6,1,512]{3,2,1,0:T(1,128)S(1)}, u32[]{:S(2)}) copy-start(f32[1,6,1,512]{3,2,1,0:T(1,128)S(1)} %collective-permute-done.22) | copy-start | bytes 36868
  114.7 15.3 %copy-start.12 = (f32[1,6,1,512]{3,2,1,0:T(1,128)}, f32[1,6,1,512]{3,2,1,0:T(1,128)S(1)}, u32[]{:S(2)}) copy-start(f32[1,6,1,512]{3,2,1,0:T(1,128)S(1)} %collective-permute-done.23) | copy-start | bytes 36868
  114.9 0.7 copy-start.1
  115.6 6.5 %collective-permute-start.25 = (f32[1,1,8,512]{3,2,1,0:T(8,128)S(1)}, f32[1,1,8,512]{3,2,1,0:T(8,128)S(1)}, u32[]{:S(2)}, u32[]{:S(2)}) collective-permute-start(f32[1,1,8,512]{3,2,1,0:T(8,128)S(1)} %get-tuple-element.50), channel_id=1, source_target_pairs={{0,2},{2,4},{4,6},{6,8},{8,10},{10,12},{12,14},{14,16},{16,18},{18... | collective-permute-start | bytes 49160 | tf_op jit(solution)/shard_map/ppermute | solution.py:17
  120.7 6.8 %collective-permute-start.24 = (f32[1,1,8,512]{3,2,1,0:T(8,128)S(1)}, f32[1,1,8,512]{3,2,1,0:T(8,128)S(1)}, u32[]{:S(2)}, u32[]{:S(2)}) collective-permute-start(f32[1,1,8,512]{3,2,1,0:T(8,128)S(1)} %get-tuple-element.51), channel_id=1, source_target_pairs={{2,0},{4,2},{6,4},{8,6},{10,8},{12,10},{14,12},{16,14},{18,16},{20... | collective-permute-start | bytes 49160 | tf_op jit(solution)/shard_map/ppermute | solution.py:20
  122.1 5.4 %copy-start.9 = (f32[1,1,8,512]{3,2,1,0:T(8,128)}, f32[1,1,8,512]{3,2,1,0:T(8,128)S(1)}, u32[]{:S(2)}) copy-start(f32[1,1,8,512]{3,2,1,0:T(8,128)S(1)} %collective-permute-done.25) | copy-start | bytes 49156
  127.5 0.6 copy-start.10
  128.1 6.1 %collective-permute-start.27 = (f32[1,6,1,512]{3,2,1,0:T(1,128)}, f32[1,6,1,512]{3,2,1,0:T(1,128)}, u32[]{:S(2)}, u32[]{:S(2)}) collective-permute-start(f32[1,6,1,512]{3,2,1,0:T(1,128)} %get-tuple-element.38), channel_id=1, source_target_pairs={{0,1},{2,3},{4,5},{6,7},{8,9},{10,11},{12,13},{14,15},{16,17},{18,... | collective-permute-start | bytes 36872 | tf_op jit(solution)/shard_map/ppermute | solution.py:17
  130.0 4.2 %collective-permute-start.26 = (f32[1,6,1,512]{3,2,1,0:T(1,128)}, f32[1,6,1,512]{3,2,1,0:T(1,128)}, u32[]{:S(2)}, u32[]{:S(2)}) collective-permute-start(f32[1,6,1,512]{3,2,1,0:T(1,128)} %get-tuple-element.39), channel_id=1, source_target_pairs={{1,0},{3,2},{5,4},{7,6},{9,8},{11,10},{13,12},{15,14},{17,16},{19,... | collective-permute-start | bytes 36872 | tf_op jit(solution)/shard_map/ppermute | solution.py:20
  136.0 18.3 %copy-start.5 = (f32[4,8,512]{2,1,0:T(8,128)S(1)}, f32[4,8,512]{2,1,0:T(8,128)}, u32[]{:S(2)}) copy-start(f32[4,8,512]{2,1,0:T(8,128)} %copy-done.4) | copy-start | bytes 196612
  140.7 23.2 %all-to-all-start.1 = ((f32[16,8,4,128]{3,1,2,0:T(8,128)}), f32[16,8,4,128]{3,1,2,0:T(8,128)}, u32[]{:S(2)}, u32[]{:S(2)}) async-start(f32[16,8,4,128]{3,1,2,0:T(8,128)} %fusion.1), calls=%async_computation.1 | async-start | bytes 524288 | tf_op jit(solution)/shard_map/all_to_all | solution.py:111
  154.3 14.8 %copy-start.7 = (f32[64,64]{1,0:T(8,128)S(1)}, f32[64,64]{1,0:T(8,128)}, u32[]{:S(2)}) copy-start(f32[64,64]{1,0:T(8,128)} %param.7) | copy-start | bytes 49156
  156.2 12.9 %copy-start.6 = (f32[64,3,64]{2,0,1:T(8,128)S(1)}, f32[64,3,64]{2,0,1:T(8,128)}, u32[]{:S(2)}) copy-start(f32[64,3,64]{2,0,1:T(8,128)} %param.8) | copy-start | bytes 147460
where the time goes:
time: 171 us; the launch traced here: 170 us
  starting transfers between devices  88.2 us (52%)
  waiting for transfers between devices  27 us (16%)
  blocking collectives  19.6 us (11%)
  other arithmetic  14.8 us (9%)
  local copies, waits for them, and re-layouts  10.7 us (6%)
  matrix products  8.18 us (5%)
    ppermute x14, starting transfers between devices, with_halo(): lax.ppermute(lax.slice_in_dim(block, block.shape[dim] - width, None, axis...  57.2 us
    all_to_all x1, blocking collectives, local(): lax.all_to_all(send_sums.reshape(n_wide, capacity, 5, cells_tile), 'wide'...  19.6 us
    ppermute x14, starting transfers between devices, with_halo(): lax.ppermute(lax.slice_in_dim(block, 0, width, axis=dim), axis, backward)  18.1 us
    ppermute x14, waiting for transfers between devices, with_halo(): lax.ppermute(lax.slice_in_dim(block, block.shape[dim] - width, None, axis...  13.5 us
    all_to_all x1, starting transfers between devices, local(): lax.all_to_all(picked.reshape(n_wide, capacity, 4, cells_tile), 'wide', s...  13 us
    all_to_all x1, waiting for transfers between devices, local(): lax.all_to_all(picked.reshape(n_wide, capacity, 4, cells_tile), 'wide', s...  7.67 us
    ppermute x14, waiting for transfers between devices, with_halo(): lax.ppermute(lax.slice_in_dim(block, 0, width, axis=dim), axis, backward)  5.9 us
  transfers between devices with their start and end apart: 29, of which 16 were waited for; matrix products, arithmetic and copies ran while one was open for 3% of the time, Pallas kernels for 0%

commit v1 on v0

v1 whole, which is shorter than its diff:
```python
import functools

import jax
import jax.numpy as jnp
from jax import lax
from jax.experimental import pallas as pl
from jax.experimental.pallas import tpu as pltpu
from jax.sharding import PartitionSpec as P

SWEEPS = 6
MESH = pl.DeviceIdType.MESH
f32 = jnp.float32
bf16 = jnp.bfloat16


def split(value):
    high = value.astype(bf16)
    return high, (value - high.astype(f32)).astype(bf16)


def dot(a, b):
    return jnp.dot(a, b, preferred_element_type=f32)


def body(
    n_wide, n_narrow, cap,
    kernel_hbm, volume_ref, velocity_ref, brick_ref, tile_ref, fluid_ref,
    drag_ref, pressure_ref, next_ref,
    kernel_buf, pieces, rows, sent_tiles, got_tiles, sent, got,
    sent_growth, got_growth, sent_next, got_next,
    first, first_z, first_gx, first_gz, press, press_z, press_gx, press_gz,
    load_sem, send_sem, recv_sem, side_send, side_recv,
):
    wide, narrow = lax.axis_index("wide"), lax.axis_index("narrow")
    blocks, particles, lanes = kernel_buf.shape
    _, cx, cz, ny = fluid_ref.shape
    nq = ny // lanes
    plane = nq * cz
    tiles = cx * plane
    slots = n_wide * cap

    load = pltpu.make_async_copy(kernel_hbm, kernel_buf, load_sem)
    load.start()

    barrier = pltpu.get_barrier_semaphore()

    def greet(step, carry):
        pl.semaphore_signal(
            barrier, inc=1, device_id=(lax.rem(wide + step, n_wide), narrow), device_id_type=MESH
        )
        return carry

    lax.fori_loop(1, n_wide, greet, 0)
    for shift in (-1, 1):
        here = (narrow > 0) if shift < 0 else (narrow < n_narrow - 1)

        @pl.when(here)
        def _():
            pl.semaphore_signal(
                barrier, inc=1, device_id=(wide, narrow + shift), device_id_type=MESH
            )

    for at_edge, index, ghosts in (
        (wide == 0, 0, (first_gx, press_gx)),
        (wide == n_wide - 1, 1, (first_gx, press_gx)),
        (narrow == 0, 0, (first_gz, press_gz)),
        (narrow == n_narrow - 1, 1, (first_gz, press_gz)),
    ):

        @pl.when(at_edge)
        def _():
            ghosts[0][index] = jnp.zeros(ghosts[0].shape[1:], f32)
            for e in range(SWEEPS):
                ghosts[1][e, index] = jnp.zeros(ghosts[1].shape[2:], f32)

    rows_b = lax.broadcasted_iota(jnp.int32, (blocks, blocks), 0)
    cols_b = lax.broadcasted_iota(jnp.int32, (blocks, blocks), 1)
    target_row = jnp.broadcast_to(brick_ref[...].astype(f32), (blocks, blocks))
    target_col = jnp.sum(jnp.where(rows_b == cols_b, target_row, 0.0), axis=1, keepdims=True)
    same = jnp.where(target_col == target_row, 1.0, 0.0)
    position_row = jnp.sum(jnp.where(rows_b < cols_b, same, 0.0), axis=0, keepdims=True)
    position_col = jnp.sum(jnp.where(cols_b < rows_b, same, 0.0), axis=1, keepdims=True)
    placed_row = target_row[:1] * cap + position_row
    placed_col = target_col * cap + position_col
    slot_col = lax.broadcasted_iota(jnp.int32, (slots, blocks), 0).astype(f32)
    place = jnp.where(slot_col == placed_row, 1.0, 0.0)
    tile_col = jnp.sum(place * tile_ref[...].astype(f32), axis=1, keepdims=True)
    sent_tiles[...] = jnp.broadcast_to(tile_col, (slots, lanes)).reshape(n_wide, cap, lanes)

    beside_z = jnp.where(narrow > 0, 1, 0) + jnp.where(narrow < n_narrow - 1, 1, 0)
    pl.semaphore_wait(barrier, n_wide - 1 + beside_z)

    def passing(phase, source, target, step):
        partner = lax.rem(wide + step, n_wide)
        return pltpu.make_async_remote_copy(
            src_ref=source.at[partner],
            dst_ref=target.at[wide],
            send_sem=send_sem.at[phase, step],
            recv_sem=recv_sem.at[phase, step],
            device_id=(partner, narrow),
            device_id_type=MESH,
        )

    def start_all(phase, source, target):
        def go(step, carry):
            passing(phase, source, target, step).start()
            return carry

        lax.fori_loop(1, n_wide, go, 0)
        target[wide] = source[wide]

    def wait_all(phase, source, target):
        def go(step, carry):
            passing(phase, source, target, step).wait_recv()
            return carry

        lax.fori_loop(1, n_wide, go, 0)

    def end_all(phase, source, target):
        def go(step, carry):
            passing(phase, source, target, step).wait_send()
            return carry

        lax.fori_loop(1, n_wide, go, 0)

    start_all(0, sent_tiles, got_tiles)

    volume = volume_ref[...]
    carried = [volume] + [volume * velocity_ref[a] for a in range(3)]
    for k in range(4):
        high = carried[k].astype(bf16).astype(f32)
        low = carried[k] - high
        rows[pl.ds(k, blocks, stride=8), :] = jnp.concatenate([high, high], axis=1)
        rows[pl.ds(4 + k, blocks, stride=8), :] = jnp.concatenate(
            [low, jnp.zeros_like(low)], axis=1
        )
    load.wait()
    group = 8

    def contract(step, carry):
        base = pl.multiple_of(step * group, group)
        weights = kernel_buf[pl.ds(base, group)]
        high, low = split(weights)
        both = jnp.concatenate([high, low], axis=1)
        pieces[pl.ds(base, group)] = both
        at = pl.ds(pl.multiple_of(base * 8, 8), group * 8)
        left = rows[at, :].reshape(group, 8, lanes).astype(bf16)
        out = lax.dot_general(
            left, both, (((2,), (1,)), ((0,), (0,))), preferred_element_type=f32
        )
        rows[at, :] = out.reshape(group * 8, lanes)
        return carry

    lax.fori_loop(0, blocks // group, contract, 0)
    own = [
        split(rows[pl.ds(k, blocks, stride=8), :] + rows[pl.ds(4 + k, blocks, stride=8), :])
        for k in range(4)
    ]
    right = jnp.concatenate(
        [jnp.concatenate([o[0] for o in own], axis=1), jnp.concatenate([o[1] for o in own], axis=1)],
        axis=0,
    )
    place = jnp.concatenate([place, place], axis=1).astype(bf16)
    in_slots = dot(place, right)
    for k in range(4):
        sent[:, k] = in_slots[:, k * lanes : (k + 1) * lanes].reshape(n_wide, cap, lanes)
    start_all(1, sent, got)

    wait_all(0, sent_tiles, got_tiles)
    order = lax.broadcasted_iota(jnp.int32, (slots, tiles), 1)
    x_of, q_of, z_of = order // plane, (order // cz) % nq, order % cz
    tile_of = ((x_of * cz + z_of) * nq + q_of).astype(f32)
    tile_slots = got_tiles[...].reshape(slots, lanes)
    selector = jnp.where(tile_slots == tile_of, 1.0, 0.0)
    turned = jnp.transpose(selector).astype(bf16)
    selector = selector.astype(bf16)
    turned = jnp.concatenate([turned, turned], axis=1)
    selector = jnp.concatenate([selector, selector], axis=1)

    fluid = [
        jnp.concatenate(
            [
                fluid_ref[a, x, :, q * lanes : (q + 1) * lanes]
                for x in range(cx)
                for q in range(nq)
            ],
            axis=0,
        )
        for a in range(3)
    ]

    wait_all(1, sent, got)
    arrived = [split(got[:, k].reshape(slots, lanes)) for k in range(4)]
    right = jnp.concatenate(
        [jnp.concatenate([o[i] for o in arrived], axis=1) for i in range(2)], axis=0
    )
    spread = dot(turned, right)
    solid = spread[:, :lanes]
    growth = (1.0 + solid) * (1.0 + solid)
    scale = 1.0 / (1.0 + growth * solid)
    provisional = [
        (fluid[a] + growth * spread[:, (a + 1) * lanes : (a + 2) * lanes]) * scale
        for a in range(3)
    ]
    void = 1.0 / (1.0 + solid)
    shape = (cx, nq, cz, lanes)
    stacked = [(void * provisional[a]).reshape(shape) for a in range(3)] + [void.reshape(shape)]

    def sides_of(e, source, source_z, ghost_x, ghost_z, fields):
        count = len(fields)
        high_rows = count * plane
        for x in range(cx):
            for i in range(count):
                source[x, i * plane : (i + 1) * plane, :] = fields[i][x].reshape(plane, lanes)
        for i in range(count):
            for side, z in ((0, 0), (1, cz - 1)):
                for x in range(cx):
                    source_z[side, (x * count + i) * nq : (x * count + i + 1) * nq, :] = fields[i][
                        x, :, z, :
                    ]

        def copies(along, side):
            if along == 0:
                src = source.at[0 if side == 0 else cx - 1]
                dst, to = ghost_x.at[1 - side], (wide + (1 if side else -1), narrow)
            else:
                src, dst = source_z.at[side], ghost_z.at[1 - side]
                to = (wide, narrow + (1 if side else -1))
            return pltpu.make_async_remote_copy(
                src_ref=src,
                dst_ref=dst,
                send_sem=side_send.at[e, along * 2 + side],
                recv_sem=side_recv.at[e, along * 2 + side],
                device_id=to,
                device_id_type=MESH,
            )

        has = (
            (wide > 0, wide < n_wide - 1),
            (narrow > 0, narrow < n_narrow - 1),
        )
        for along in range(2):
            for side in range(2):

                @pl.when(has[along][side])
                def _():
                    copies(along, side).start()

        lane = lax.broadcasted_iota(jnp.int32, shape, 3)
        row = lax.broadcasted_iota(jnp.int32, shape, 2)
        zero = jnp.zeros((cx, 1, cz, lanes), f32)
        in_y = []
        for p in fields:
            up = pltpu.roll(p, lanes - 1, 3)
            down = pltpu.roll(p, 1, 3)
            up = jnp.where(lane == lanes - 1, jnp.concatenate([up[:, 1:], zero], axis=1), up)
            down = jnp.where(lane == 0, jnp.concatenate([zero, down[:, :-1]], axis=1), down)
            in_y.append((up, down))
        for along in range(2):
            for side in range(2):

                @pl.when(has[along][1 - side])
                def _():
                    copies(along, side).wait_recv()

        result = []
        for i, p in enumerate(fields):
            low = ghost_x[0, i * plane : (i + 1) * plane, :].reshape((1,) + shape[1:])
            high = ghost_x[1, i * plane : (i + 1) * plane, :].reshape((1,) + shape[1:])

            def row_ghost(side):
                return jnp.concatenate(
                    [
                        jnp.broadcast_to(
                            ghost_z[side, (x * count + i) * nq + q : (x * count + i) * nq + q + 1, :],
                            (cz, lanes),
                        )
                        for x in range(cx)
                        for q in range(nq)
                    ],
                    axis=0,
                ).reshape(shape)

            z_up = jnp.where(row == cz - 1, row_ghost(1), pltpu.roll(p, cz - 1, 2))
            z_down = jnp.where(row == 0, row_ghost(0), pltpu.roll(p, 1, 2))
            result.append(
                (
                    jnp.concatenate([p[1:], high], axis=0),
                    jnp.concatenate([low, p[:-1]], axis=0),
                    z_up,
                    z_down,
                    in_y[i][0],
                    in_y[i][1],
                )
            )
        for along in range(2):
            for side in range(2):

                @pl.when(has[along][side])
                def _():
                    copies(along, side).wait_send()

        return result

    beside = sides_of(0, first, first_z, first_gx, first_gz, stacked)

    def give_back(values, target, start):
        wide_values = [split(v) for v in values]
        right = jnp.concatenate(
            [jnp.concatenate([o[i] for o in wide_values], axis=1) for i in range(2)], axis=0
        )
        picked = dot(selector, right)
        for k in range(len(values)):
            target[:, start + k] = picked[:, k * lanes : (k + 1) * lanes].reshape(
                n_wide, cap, lanes
            )

    give_back([growth], sent_growth, 0)
    start_all(2, sent_growth, got_growth)

    source = -0.5 * (
        beside[0][0] - beside[0][1] + beside[1][2] - beside[1][3] + beside[2][4] - beside[2][5]
    )
    here_void = stacked[3]
    weights = [0.5 * (here_void + beside[3][i]) for i in range(6)]
    diagonal = weights[0] + weights[1] + weights[2] + weights[3] + weights[4] + weights[5]
    inverse = 1.0 / diagonal
    weights = [w * inverse for w in weights]
    source = source * inverse
    pressure = source
    for sweep in range(SWEEPS):
        around = sides_of(
            1 + sweep,
            press.at[sweep],
            press_z.at[sweep],
            press_gx.at[sweep],
            press_gz.at[sweep],
            [pressure],
        )[0]
        if sweep < SWEEPS - 1:
            total = source
            for i in range(6):
                total = total + weights[i] * around[i]
            pressure = total
    steps = [around[0] - around[1], around[2] - around[3], around[4] - around[5]]
    following = [provisional[a] - 0.5 * steps[a].reshape(tiles, lanes) for a in range(3)]
    give_back([growth * v for v in following], sent_next, 0)
    start_all(3, sent_next, got_next)

    for x in range(cx):
        for q in range(nq):
            cut = slice(q * lanes, (q + 1) * lanes)
            at = (x * nq + q) * cz
            pressure_ref[x, :, cut] = pressure[x, q]
            for a in range(3):
                next_ref[a, x, :, cut] = following[a][at : at + cz]

    slot_row = lax.broadcasted_iota(jnp.int32, (blocks, slots), 1).astype(f32)
    back = jnp.where(slot_row == placed_col, 1.0, 0.0).astype(bf16)

    def place_back(target, k, row):
        high, low = split(target[:, k].reshape(slots, lanes))
        out = dot(back, jnp.concatenate([high, low], axis=1))
        rows[pl.ds(row, blocks, stride=8), :] = out[:, :lanes]
        rows[pl.ds(4 + row, blocks, stride=8), :] = out[:, lanes:]

    wait_all(2, sent_growth, got_growth)
    place_back(got_growth, 0, 3)
    wait_all(3, sent_next, got_next)
    for k in range(3):
        place_back(got_next, k, k)

    def sample(step, carry):
        base = pl.multiple_of(step * group, group)
        at = pl.ds(pl.multiple_of(base * 8, 8), group * 8)
        left = rows[at, :].reshape(group, 8, lanes).astype(bf16)
        out = lax.dot_general(
            left,
            pieces[pl.ds(base, group)],
            (((2,), (2,)), ((0,), (0,))),
            preferred_element_type=f32,
        )
        rows[at, :] = out.reshape(group * 8, lanes)
        return carry

    lax.fori_loop(0, blocks // group, sample, 0)

    def sampled(k):
        top = rows[pl.ds(k, blocks, stride=8), :]
        low = rows[pl.ds(4 + k, blocks, stride=8), :]
        return (top + low)[:, :particles] + pltpu.roll(top, particles, 1)[:, :particles]

    fourth = sampled(3)
    for k in range(3):
        drag_ref[k] = volume * sampled(k) - carried[1 + k] * fourth

    for phase, source, target in (
        (0, sent_tiles, got_tiles),
        (1, sent, got),
        (2, sent_growth, got_growth),
        (3, sent_next, got_next),
    ):
        end_all(phase, source, target)


def solution(mesh):
    n_wide, n_narrow = mesh.shape["wide"], mesh.shape["narrow"]

    def local(kernel, volume, velocity, block_brick, block_tile, fluid_velocity):
        blocks, particles, lanes = kernel.shape
        _, cx, cz, ny = fluid_velocity.shape
        cap = max(2, (2 * blocks + n_wide - 1) // n_wide)
        cap = (cap + 7) // 8 * 8
        nq = ny // lanes
        plane = nq * cz
        vmem = pltpu.VMEM
        any_spec = pl.BlockSpec(memory_space=pl.ANY)
        vmem_spec = pl.BlockSpec(memory_space=pltpu.VMEM)
        flux = [
            vmem((n_wide, cap, lanes), f32),
            vmem((n_wide, cap, lanes), f32),
            vmem((n_wide, 4, cap, lanes), f32),
            vmem((n_wide, 4, cap, lanes), f32),
            vmem((n_wide, 1, cap, lanes), f32),
            vmem((n_wide, 1, cap, lanes), f32),
            vmem((n_wide, 3, cap, lanes), f32),
            vmem((n_wide, 3, cap, lanes), f32),
        ]
        halo = [
            vmem((cx, 4 * plane, lanes), f32),
            vmem((2, 4 * cx * nq, lanes), f32),
            vmem((2, 4 * plane, lanes), f32),
            vmem((2, 4 * cx * nq, lanes), f32),
            vmem((SWEEPS, cx, plane, lanes), f32),
            vmem((SWEEPS, 2, cx * nq, lanes), f32),
            vmem((SWEEPS, 2, plane, lanes), f32),
            vmem((SWEEPS, 2, cx * nq, lanes), f32),
        ]
        drag, pressure, following = pl.pallas_call(
            functools.partial(body, n_wide, n_narrow, cap),
            out_shape=(
                jax.ShapeDtypeStruct((3, blocks, particles), f32),
                jax.ShapeDtypeStruct((cx, cz, ny), f32),
                jax.ShapeDtypeStruct((3, cx, cz, ny), f32),
            ),
            in_specs=[any_spec] + [vmem_spec] * 5,
            out_specs=(vmem_spec,) * 3,
            scratch_shapes=[
                vmem((blocks, particles, lanes), f32),
                vmem((blocks, 2 * particles, lanes), bf16),
                vmem((blocks * 8, lanes), f32),
            ]
            + flux
            + halo
            + [
                pltpu.SemaphoreType.DMA,
                pltpu.SemaphoreType.DMA((4, n_wide)),
                pltpu.SemaphoreType.DMA((4, n_wide)),
                pltpu.SemaphoreType.DMA((SWEEPS + 1, 4)),
                pltpu.SemaphoreType.DMA((SWEEPS + 1, 4)),
            ],
            compiler_params=pltpu.CompilerParams(
                collective_id=0, has_side_effects=True, vmem_limit_bytes=40 * 1024 * 1024
            ),
        )(
            kernel,
            volume,
            jnp.transpose(velocity, (1, 0, 2)),
            block_brick.reshape(1, blocks),
            block_tile.reshape(1, blocks),
            fluid_velocity,
        )
        return jnp.transpose(drag, (1, 0, 2)), pressure, following

    return jax.shard_map(
        local,
        mesh=mesh,
        in_specs=(
            P(("wide", "narrow"), None, None),
            P(("wide", "narrow"), None),
            P(("wide", "narrow"), None, None),
            P(("wide", "narrow"), None),
            P(("wide", "narrow")),
            P(None, "wide", "narrow", None),
        ),
        out_specs=(
            P(("wide", "narrow"), None, None),
            P("wide", "narrow", None),
            P(None, "wide", "narrow", None),
        ),
        check_vma=False,
    )
```

time: 171 us -> 61.1 us (0.36)
  starting transfers between devices: 88.2 us -> 0 us
  Pallas kernels: 0 us -> 52.8 us
  waiting for transfers between devices: 27 us -> 0 us
  blocking collectives: 19.6 us -> 0 us
  other arithmetic: 14.8 us -> 0 us
  matrix products: 8.18 us -> 0 us
  local copies, waits for them, and re-layouts: 10.7 us -> 7.42 us
    ppermute x28 -> x0, starting transfers between devices: 75.3 us -> none  [the longest x14 57.2 us: with_halo(): lax.ppermute(lax.slice_in_dim(block, block.shape[dim] - width, None, axis...]
    pallas_call x0 -> x1, Pallas kernels: none -> 52.8 us  [local(): pl.pallas_call(functools.partial(body, n_wide, n_narrow, cap), out_shape=...]
    all_to_all x1 -> x0, blocking collectives: 19.6 us -> none  [local(): lax.all_to_all(send_sums.reshape(n_wide, capacity, 5, cells_tile), 'wide'...]
    ppermute x28 -> x0, waiting for transfers between devices: 19.4 us -> none  [the longest x14 13.5 us: with_halo(): lax.ppermute(lax.slice_in_dim(block, block.shape[dim] - width, None, axis...]
    all_to_all x1 -> x0, starting transfers between devices: 13 us -> none  [local(): lax.all_to_all(picked.reshape(n_wide, capacity, 4, cells_tile), 'wide', s...]
    dot_general x4 -> x0, matrix products: 8.18 us -> none  [the longest x1 3.35 us: local(): jnp.einsum('bkc,bpc->bkp', block_fields, kernel, precision=highest)]
    all_to_all x1 -> x0, waiting for transfers between devices: 7.67 us -> none  [local(): lax.all_to_all(picked.reshape(n_wide, capacity, 4, cells_tile), 'wide', s...]
    unnamed x31 -> x15, local copies, waits for them, and re-layouts: 1.87 us -> 7.42 us
  transfers between devices with their start and end apart: 29 -> 0, of which waited for: 16 -> 0; matrix products, arithmetic and copies ran while one was open for 3% -> 0% of each run, Pallas kernels for 0% -> 0%
where the time goes in v1:
time: 61.1 us; the launch traced here: 60.9 us
  Pallas kernels  52.8 us (86%)
  local copies, waits for them, and re-layouts  7.42 us (12%)
  between operations  0.65 us (1%)
    pallas_call x1, Pallas kernels, local(): pl.pallas_call(functools.partial(body, n_wide, n_narrow, cap), out_shape=...  52.8 us
    unnamed x15, local copies, waits for them, and re-layouts  7.42 us

profile of v1, /device:TPU:0, one launch (start us, length us, event | category | flops | bytes accessed | tf_op | source)
XLA Modules:
  0.0 60.9 jit_solution(15795363974543290808)
XLA Ops:
  0.6 0.0 copy-start
  0.6 1.6 %copy-done = f32[64,64,128]{2,1,0:T(8,128)S(1)} copy-done((f32[64,64,128]{2,1,0:T(8,128)S(1)}, f32[64,64,128]{2,1,0:T(8,128)}, u32[]{:S(2)}) %copy-start) | copy-done | bytes 2097176
  2.2 0.0 copy-start.1
  2.2 0.9 %copy-done.1 = f32[3,4,8,512]{3,2,1,0:T(8,128)S(1)} copy-done((f32[3,4,8,512]{3,2,1,0:T(8,128)S(1)}, f32[3,4,8,512]{3,2,1,0:T(8,128)}, u32[]{:S(2)}) %copy-start.1) | copy-done | bytes 196632
  3.2 0.0 copy-start.2
  3.2 0.9 %copy-done.2 = f32[64,3,64]{2,0,1:T(8,128)S(1)} copy-done((f32[64,3,64]{2,0,1:T(8,128)S(1)}, f32[64,3,64]{2,0,1:T(8,128)}, u32[]{:S(2)}) %copy-start.2) | copy-done | bytes 49176
  4.0 0.0 copy-start.3
  4.0 0.8 %copy-done.3 = f32[64,64]{1,0:T(8,128)S(1)} copy-done((f32[64,64]{1,0:T(8,128)S(1)}, f32[64,64]{1,0:T(8,128)}, u32[]{:S(2)}) %copy-start.3) | copy-done | bytes 16408
  4.8 0.0 copy-start.4
  4.8 0.7 %copy-done.4 = s32[64,1]{0,1:T(1,128)S(1)} copy-done((s32[64,1]{0,1:T(1,128)S(1)}, s32[64,1]{0,1:T(1,128)}, u32[]{:S(2)}) %copy-start.4) | copy-done | bytes 280
  5.5 0.0 copy-start.5
  5.5 0.7 %copy-done.5 = s32[64]{0:T(128)S(1)} copy-done((s32[64]{0:T(128)S(1)}, s32[64]{0:T(128)}, u32[]{:S(2)}) %copy-start.5) | copy-done | bytes 280
  6.1 52.8 %shard_map.85 = (f32[3,64,64]{2,1,0:T(8,128)S(1)}, f32[4,8,512]{2,1,0:T(8,128)S(1)}, f32[3,4,8,512]{3,2,1,0:T(8,128)S(1)}) custom-call(f32[64,64,128]{2,1,0:T(8,128)S(1)} %copy-done, f32[64,64]{1,0:T(8,128)S(1)} %copy-done.3, f32[3,64,64]{2,1,0:T(8,128)S(1)} %bitcast.4, s32[1,64]{1,0:T(1,128)S(1)} %bitcast.6, s32[1,64]{1,0:T(1,128)S(1)} %bitcast.7, ...), custom_call_target="tpu_custom_call" | custom-call | tf_op jit(solution)/shard_map/pallas_call | solution.py:439
  58.9 0.6 %copy.12 = f32[64,3,64]{2,0,1:T(8,128)} copy(f32[64,3,64]{2,0,1:T(8,128)S(1)} %bitcast.5) | data formatting | bytes 98304
  59.6 0.6 %copy.13 = f32[4,8,512]{2,1,0:T(8,128)} copy(f32[4,8,512]{2,1,0:T(8,128)S(1)} %get-tuple-element.13) | data formatting | bytes 131072
  60.2 0.7 %copy.14 = f32[3,4,8,512]{3,2,1,0:T(8,128)} copy(f32[3,4,8,512]{3,2,1,0:T(8,128)S(1)} %get-tuple-element.14) | data formatting | bytes 393216
Async XLA Ops:
  0.6 1.6 %copy-start = (f32[64,64,128]{2,1,0:T(8,128)S(1)}, f32[64,64,128]{2,1,0:T(8,128)}, u32[]{:S(2)}) copy-start(f32[64,64,128]{2,1,0:T(8,128)} %kernel_hbm.1) | copy-start | bytes 6291460
  2.2 0.9 %copy-start.1 = (f32[3,4,8,512]{3,2,1,0:T(8,128)S(1)}, f32[3,4,8,512]{3,2,1,0:T(8,128)}, u32[]{:S(2)}) copy-start(f32[3,4,8,512]{3,2,1,0:T(8,128)} %fluid_ref.1) | copy-start | bytes 589828
  3.2 0.9 %copy-start.2 = (f32[64,3,64]{2,0,1:T(8,128)S(1)}, f32[64,3,64]{2,0,1:T(8,128)}, u32[]{:S(2)}) copy-start(f32[64,3,64]{2,0,1:T(8,128)} %param.8) | copy-start | bytes 147460
  4.0 0.8 %copy-start.3 = (f32[64,64]{1,0:T(8,128)S(1)}, f32[64,64]{1,0:T(8,128)}, u32[]{:S(2)}) copy-start(f32[64,64]{1,0:T(8,128)} %volume_ref.1) | copy-start | bytes 49156
  4.8 0.7 %copy-start.4 = (s32[64,1]{0,1:T(1,128)S(1)}, s32[64,1]{0,1:T(1,128)}, u32[]{:S(2)}) copy-start(s32[64,1]{0,1:T(1,128)} %param.9) | copy-start | bytes 772
  5.5 0.7 %copy-start.5 = (s32[64]{0:T(128)S(1)}, s32[64]{0:T(128)}, u32[]{:S(2)}) copy-start(s32[64]{0:T(128)} %param.10) | copy-start | bytes 772

commit v2 on v1

--- a/solution.py
+++ b/solution.py
@@ -24,9 +24,9 @@
 
 def body(
     n_wide, n_narrow, cap,
-    kernel_hbm, volume_ref, velocity_ref, brick_ref, tile_ref, fluid_ref,
+    kernel_hbm, volume_hbm, velocity_hbm, brick_hbm, tile_hbm, fluid_hbm,
     drag_ref, pressure_ref, next_ref,
-    kernel_buf, pieces, rows, sent_tiles, got_tiles, sent, got,
+    kernel_buf, volume_ref, velocity_ref, brick_ref, tile_ref, fluid_ref, pieces, rows, sent_tiles, got_tiles, sent, got,
     sent_growth, got_growth, sent_next, got_next,
     first, first_z, first_gx, first_gz, press, press_z, press_gx, press_gz,
     load_sem, send_sem, recv_sem, side_send, side_recv,
@@ -39,8 +39,21 @@
     tiles = cx * plane
     slots = n_wide * cap
 
-    load = pltpu.make_async_copy(kernel_hbm, kernel_buf, load_sem)
-    load.start()
+    loads = [
+        pltpu.make_async_copy(here, there, load_sem.at[i])
+        for i, (here, there) in enumerate(
+            (
+                (brick_hbm, brick_ref),
+                (tile_hbm, tile_ref),
+                (volume_hbm, volume_ref),
+                (velocity_hbm, velocity_ref),
+                (kernel_hbm, kernel_buf),
+                (fluid_hbm, fluid_ref),
+            )
+        )
+    ]
+    for load in loads:
+        load.start()
 
     barrier = pltpu.get_barrier_semaphore()
 
@@ -73,6 +86,8 @@
             for e in range(SWEEPS):
                 ghosts[1][e, index] = jnp.zeros(ghosts[1].shape[2:], f32)
 
+    loads[0].wait()
+    loads[1].wait()
     rows_b = lax.broadcasted_iota(jnp.int32, (blocks, blocks), 0)
     cols_b = lax.broadcasted_iota(jnp.int32, (blocks, blocks), 1)
     target_row = jnp.broadcast_to(brick_ref[...].astype(f32), (blocks, blocks))
@@ -125,6 +140,8 @@
 
     start_all(0, sent_tiles, got_tiles)
 
+    loads[2].wait()
+    loads[3].wait()
     volume = volume_ref[...]
     carried = [volume] + [volume * velocity_ref[a] for a in range(3)]
     for k in range(4):
@@ -134,7 +151,7 @@
         rows[pl.ds(4 + k, blocks, stride=8), :] = jnp.concatenate(
             [low, jnp.zeros_like(low)], axis=1
         )
-    load.wait()
+    loads[4].wait()
     group = 8
 
     def contract(step, carry):
@@ -177,6 +194,7 @@
     turned = jnp.concatenate([turned, turned], axis=1)
     selector = jnp.concatenate([selector, selector], axis=1)
 
+    loads[5].wait()
     fluid = [
         jnp.concatenate(
             [
@@ -401,6 +419,15 @@
         (3, sent_next, got_next),
     ):
         end_all(phase, source, target)
+
+
+def hand_over(*refs):
+    sources, targets, sems = refs[:3], refs[3:6], refs[6]
+    copies = [pltpu.make_async_copy(sources[i], targets[i], sems.at[i]) for i in range(3)]
+    for copy in copies:
+        copy.start()
+    for copy in copies:
+        copy.wait()
 
 
 def solution(mesh):
@@ -443,24 +470,29 @@
                 jax.ShapeDtypeStruct((cx, cz, ny), f32),
                 jax.ShapeDtypeStruct((3, cx, cz, ny), f32),
             ),
-            in_specs=[any_spec] + [vmem_spec] * 5,
+            in_specs=[any_spec] * 6,
             out_specs=(vmem_spec,) * 3,
             scratch_shapes=[
                 vmem((blocks, particles, lanes), f32),
+                vmem((blocks, particles), f32),
+                vmem((3, blocks, particles), f32),
+                vmem((1, blocks), jnp.int32),
+                vmem((1, blocks), jnp.int32),
+                vmem((3, cx, cz, ny), f32),
                 vmem((blocks, 2 * particles, lanes), bf16),
                 vmem((blocks * 8, lanes), f32),
             ]
             + flux
             + halo
             + [
-                pltpu.SemaphoreType.DMA,
+                pltpu.SemaphoreType.DMA((6,)),
                 pltpu.SemaphoreType.DMA((4, n_wide)),
                 pltpu.SemaphoreType.DMA((4, n_wide)),
                 pltpu.SemaphoreType.DMA((SWEEPS + 1, 4)),
                 pltpu.SemaphoreType.DMA((SWEEPS + 1, 4)),
             ],
             compiler_params=pltpu.CompilerParams(
-                collective_id=0, has_side_effects=True, vmem_limit_bytes=40 * 1024 * 1024
+                collective_id=0, has_side_effects=True, vmem_limit_bytes=60 * 1024 * 1024
             ),
         )(
             kernel,
@@ -470,6 +502,14 @@
             block_tile.reshape(1, blocks),
             fluid_velocity,
         )
+        results = (drag, pressure, following)
+        drag, pressure, following = pl.pallas_call(
+            hand_over,
+            out_shape=tuple(jax.ShapeDtypeStruct(r.shape, r.dtype) for r in results),
+            in_specs=[any_spec] * 3,
+            out_specs=(any_spec,) * 3,
+            scratch_shapes=[pltpu.SemaphoreType.DMA((3,))],
+        )(*results)
         return jnp.transpose(drag, (1, 0, 2)), pressure, following
 
     return jax.shard_map(

time: 61.1 us -> 65.6 us (1.074)
  Pallas kernels: 52.8 us -> 64.8 us
  local copies, waits for them, and re-layouts: 7.42 us -> 0 us
    pallas_call x0 -> x1, Pallas kernels: none -> 12 us  [local(): pl.pallas_call(hand_over, out_shape=tuple((jax.ShapeDtypeStruct(r.shape,...]
    unnamed x15 -> x0, local copies, waits for them, and re-layouts: 7.42 us -> none
where the time goes in v2:
time: 65.6 us; the launch traced here: 65.5 us
  Pallas kernels  64.8 us (99%)
    pallas_call x1, Pallas kernels, local(): pl.pallas_call(functools.partial(body, n_wide, n_narrow, cap), out_shape=...  52.8 us
    pallas_call x1, Pallas kernels, local(): pl.pallas_call(hand_over, out_shape=tuple((jax.ShapeDtypeStruct(r.shape,...  12 us

profile of v2, /device:TPU:0, one launch (start us, length us, event | category | flops | bytes accessed | tf_op | source)
XLA Modules:
  0.0 65.5 jit_solution(16582152926170582293)
XLA Ops:
  0.6 52.8 %shard_map.85 = (f32[3,64,64]{2,1,0:T(8,128)}, f32[4,8,512]{2,1,0:T(8,128)}, f32[3,4,8,512]{3,2,1,0:T(8,128)}) custom-call(f32[64,64,128]{2,1,0:T(8,128)} %kernel_hbm.1, f32[64,64]{1,0:T(8,128)} %volume_hbm.1, f32[3,64,64]{2,1,0:T(8,128)} %bitcast.4, s32[1,64]{1,0:T(1,128)} %bitcast.5, s32[1,64]{1,0:T(1,128)} %bitcast.6, f32[3,4,8,512]{3,2,1,0:T(8,128)} %fluid_hbm.1), custom_call_target="tpu_custom_call" | custom-call | tf_op jit(solution)/shard_map/pallas_call | solution.py:466
  53.4 12.0 %shard_map.86 = (f32[3,64,64]{2,1,0:T(8,128)}, f32[4,8,512]{2,1,0:T(8,128)}, f32[3,4,8,512]{3,2,1,0:T(8,128)}) custom-call(f32[3,64,64]{2,1,0:T(8,128)} %get-tuple-element.9.refs_0_, f32[4,8,512]{2,1,0:T(8,128)} %get-tuple-element.10.refs_1_, f32[3,4,8,512]{3,2,1,0:T(8,128)} %get-tuple-element.11.refs_2_), custom_call_target="tpu_custom_call" | custom-call | tf_op jit(solution)/shard_map/pallas_call | solution.py:506

commit v3 on v2

--- a/solution.py
+++ b/solution.py
@@ -8,6 +8,8 @@
 from jax.sharding import PartitionSpec as P
 
 SWEEPS = 6
+DEPTH = 3
+DIRECTIONS = ((-1, 0), (1, 0), (0, -1), (0, 1), (-1, -1), (-1, 1), (1, -1), (1, 1))
 MESH = pl.DeviceIdType.MESH
 f32 = jnp.float32
 bf16 = jnp.bfloat16
@@ -28,7 +30,7 @@
     drag_ref, pressure_ref, next_ref,
     kernel_buf, volume_ref, velocity_ref, brick_ref, tile_ref, fluid_ref, pieces, rows, sent_tiles, got_tiles, sent, got,
     sent_growth, got_growth, sent_next, got_next,
-    first, first_z, first_gx, first_gz, press, press_z, press_gx, press_gz,
+    near_x, near_gx, near_z, near_gz, deep, deep_gx, deep_gz, corner, corner_g,
     load_sem, send_sem, recv_sem, side_send, side_recv,
 ):
     wide, narrow = lax.axis_index("wide"), lax.axis_index("narrow")
@@ -64,27 +66,51 @@
         return carry
 
     lax.fori_loop(1, n_wide, greet, 0)
-    for shift in (-1, 1):
-        here = (narrow > 0) if shift < 0 else (narrow < n_narrow - 1)
-
-        @pl.when(here)
+    z_tiles = near_gz.shape[0] + 1
+
+    def exists(dx, dz):
+        inside = (wide + dx >= 0) & (wide + dx < n_wide)
+        return inside & (narrow + dz >= 0) & (narrow + dz < n_narrow)
+
+    for dx, dz in DIRECTIONS:
+        if dz:
+
+            @pl.when(exists(dx, dz))
+            def _():
+                pl.semaphore_signal(
+                    barrier, inc=1, device_id=(wide + dx, narrow + dz), device_id_type=MESH
+                )
+
+    def lands_x(dx):
+        return 0 if dx > 0 else 1
+
+    def lands_z(dz):
+        return 0 if dz > 0 or z_tiles == 2 else 1
+
+    for dx, dz in DIRECTIONS:
+        if dz and z_tiles == 2:
+            absent = jnp.logical_not(exists(-dx, 0)) if dx else None
+            if dx and dz < 0:
+                continue
+        else:
+            absent = jnp.logical_not(exists(-dx, -dz))
+        if absent is None:
+            continue
+
+        @pl.when(absent)
         def _():
-            pl.semaphore_signal(
-                barrier, inc=1, device_id=(wide, narrow + shift), device_id_type=MESH
-            )
-
-    for at_edge, index, ghosts in (
-        (wide == 0, 0, (first_gx, press_gx)),
-        (wide == n_wide - 1, 1, (first_gx, press_gx)),
-        (narrow == 0, 0, (first_gz, press_gz)),
-        (narrow == n_narrow - 1, 1, (first_gz, press_gz)),
-    ):
-
-        @pl.when(at_edge)
-        def _():
-            ghosts[0][index] = jnp.zeros(ghosts[0].shape[1:], f32)
-            for e in range(SWEEPS):
-                ghosts[1][e, index] = jnp.zeros(ghosts[1].shape[2:], f32)
+            events = deep.shape[0]
+            if dz == 0:
+                near_gx[lands_x(dx)] = jnp.zeros(near_gx.shape[1:], f32)
+                for e in range(events):
+                    deep_gx[e, lands_x(dx)] = jnp.zeros(deep_gx.shape[2:], f32)
+            elif dx == 0:
+                near_gz[lands_z(dz)] = jnp.zeros(near_gz.shape[1:], f32)
+                for e in range(events):
+                    deep_gz[e, lands_z(dz)] = jnp.zeros(deep_gz.shape[2:], f32)
+            else:
+                for e in range(events):
+                    corner_g[e, lands_x(dx), lands_z(dz)] = jnp.zeros(corner_g.shape[3:], f32)
 
     loads[0].wait()
     loads[1].wait()
@@ -102,8 +128,9 @@
     tile_col = jnp.sum(place * tile_ref[...].astype(f32), axis=1, keepdims=True)
     sent_tiles[...] = jnp.broadcast_to(tile_col, (slots, lanes)).reshape(n_wide, cap, lanes)
 
+    beside_x = jnp.where(wide > 0, 1, 0) + jnp.where(wide < n_wide - 1, 1, 0)
     beside_z = jnp.where(narrow > 0, 1, 0) + jnp.where(narrow < n_narrow - 1, 1, 0)
-    pl.semaphore_wait(barrier, n_wide - 1 + beside_z)
+    pl.semaphore_wait(barrier, n_wide - 1 + beside_z * (1 + beside_x))
 
     def passing(phase, source, target, step):
         partner = lax.rem(wide + step, n_wide)
@@ -221,106 +248,13 @@
         for a in range(3)
     ]
     void = 1.0 / (1.0 + solid)
-    shape = (cx, nq, cz, lanes)
-    stacked = [(void * provisional[a]).reshape(shape) for a in range(3)] + [void.reshape(shape)]
-
-    def sides_of(e, source, source_z, ghost_x, ghost_z, fields):
-        count = len(fields)
-        high_rows = count * plane
-        for x in range(cx):
-            for i in range(count):
-                source[x, i * plane : (i + 1) * plane, :] = fields[i][x].reshape(plane, lanes)
-        for i in range(count):
-            for side, z in ((0, 0), (1, cz - 1)):
-                for x in range(cx):
-                    source_z[side, (x * count + i) * nq : (x * count + i + 1) * nq, :] = fields[i][
-                        x, :, z, :
-                    ]
-
-        def copies(along, side):
-            if along == 0:
-                src = source.at[0 if side == 0 else cx - 1]
-                dst, to = ghost_x.at[1 - side], (wide + (1 if side else -1), narrow)
-            else:
-                src, dst = source_z.at[side], ghost_z.at[1 - side]
-                to = (wide, narrow + (1 if side else -1))
-            return pltpu.make_async_remote_copy(
-                src_ref=src,
-                dst_ref=dst,
-                send_sem=side_send.at[e, along * 2 + side],
-                recv_sem=side_recv.at[e, along * 2 + side],
-                device_id=to,
-                device_id_type=MESH,
-            )
-
-        has = (
-            (wide > 0, wide < n_wide - 1),
-            (narrow > 0, narrow < n_narrow - 1),
-        )
-        for along in range(2):
-            for side in range(2):
-
-                @pl.when(has[along][side])
-                def _():
-                    copies(along, side).start()
-
-        lane = lax.broadcasted_iota(jnp.int32, shape, 3)
-        row = lax.broadcasted_iota(jnp.int32, shape, 2)
-        zero = jnp.zeros((cx, 1, cz, lanes), f32)
-        in_y = []
-        for p in fields:
-            up = pltpu.roll(p, lanes - 1, 3)
-            down = pltpu.roll(p, 1, 3)
-            up = jnp.where(lane == lanes - 1, jnp.concatenate([up[:, 1:], zero], axis=1), up)
-            down = jnp.where(lane == 0, jnp.concatenate([zero, down[:, :-1]], axis=1), down)
-            in_y.append((up, down))
-        for along in range(2):
-            for side in range(2):
-
-                @pl.when(has[along][1 - side])
-                def _():
-                    copies(along, side).wait_recv()
-
-        result = []
-        for i, p in enumerate(fields):
-            low = ghost_x[0, i * plane : (i + 1) * plane, :].reshape((1,) + shape[1:])
-            high = ghost_x[1, i * plane : (i + 1) * plane, :].reshape((1,) + shape[1:])
-
-            def row_ghost(side):
-                return jnp.concatenate(
-                    [
-                        jnp.broadcast_to(
-                            ghost_z[side, (x * count + i) * nq + q : (x * count + i) * nq + q + 1, :],
-                            (cz, lanes),
-                        )
-                        for x in range(cx)
-                        for q in range(nq)
-                    ],
-                    axis=0,
-                ).reshape(shape)
-
-            z_up = jnp.where(row == cz - 1, row_ghost(1), pltpu.roll(p, cz - 1, 2))
-            z_down = jnp.where(row == 0, row_ghost(0), pltpu.roll(p, 1, 2))
-            result.append(
-                (
-                    jnp.concatenate([p[1:], high], axis=0),
-                    jnp.concatenate([low, p[:-1]], axis=0),
-                    z_up,
-                    z_down,
-                    in_y[i][0],
-                    in_y[i][1],
-                )
-            )
-        for along in range(2):
-            for side in range(2):
-
-                @pl.when(has[along][side])
-                def _():
-                    copies(along, side).wait_send()
-
-        return result
-
-    beside = sides_of(0, first, first_z, first_gx, first_gz, stacked)
+    shape = (nq, cz, lanes)
+
+    def planes_of(value):
+        return [value[x * plane : (x + 1) * plane].reshape(shape) for x in range(cx)]
+
+    own_flux = [planes_of(void * provisional[a]) for a in range(3)]
+    own_void = planes_of(void)
 
     def give_back(values, target, start):
         wide_values = [split(v) for v in values]
@@ -333,35 +267,226 @@
                 n_wide, cap, lanes
             )
 
+
+    def ship(e, i, src, dst):
+        dx, dz = DIRECTIONS[i]
+        return pltpu.make_async_remote_copy(
+            src_ref=src,
+            dst_ref=dst,
+            send_sem=side_send.at[e, i],
+            recv_sem=side_recv.at[e, i],
+            device_id=(wide + dx, narrow + dz),
+            device_id_type=MESH,
+        )
+
+    def near_copy(i):
+        dx, dz = DIRECTIONS[i]
+        if dz == 0:
+            return ship(0, i, near_x.at[0 if dx < 0 else 1], near_gx.at[lands_x(dx)])
+        return ship(0, i, near_z, near_gz.at[lands_z(dz)])
+
+    def deep_copy(e, i):
+        dx, dz = DIRECTIONS[i]
+        if dz == 0:
+            start = 0 if dx < 0 else cx - DEPTH
+            return ship(
+                e + 1, i, deep.at[e, pl.ds(start, DEPTH)], deep_gx.at[e, lands_x(dx)]
+            )
+        if dx == 0:
+            return ship(e + 1, i, deep.at[e], deep_gz.at[e, lands_z(dz)])
+        return ship(
+            e + 1,
+            i,
+            corner.at[e, 0 if dx < 0 else 1, 0 if dz < 0 else 1],
+            corner_g.at[e, lands_x(dx), lands_z(dz)],
+        )
+
+    def each(directions, make, act, receiving=False):
+        for i in directions:
+            dx, dz = DIRECTIONS[i]
+
+            @pl.when(exists(-dx, -dz) if receiving else exists(dx, dz))
+            def _():
+                getattr(make(i), act)()
+
+    corner_spots = [(d, r) for d in range(1, DEPTH) for r in range(1, DEPTH + 1 - d)]
+
+    def store_deep(e, planes):
+        for x in range(cx):
+            deep[e, x] = planes[x].reshape(plane, lanes)
+        for sx in range(2):
+            for sz in range(2):
+                for n, (d, r) in enumerate(corner_spots):
+                    x = d - 1 if sx == 0 else cx - d
+                    z = r - 1 if sz == 0 else cz - r
+                    corner[e, sx, sz, n * nq : (n + 1) * nq, :] = planes[x][:, z, :]
+
+    row = lax.broadcasted_iota(jnp.int32, shape, 1)
+
+    def tiles_from(own, others):
+        if z_tiles == 2:
+            first = narrow == 0
+            return jnp.stack([jnp.where(first, own, others[0]), jnp.where(first, others[0], own)])
+        return jnp.stack([others[0], own, others[1]])
+
+    def own_of(value):
+        if z_tiles == 2:
+            return jnp.where(narrow == 0, value[0], value[1])
+        return value[1]
+
+    def corner_tile(e, side, which, d):
+        tile = jnp.zeros(shape, f32)
+        for n, (far, r) in enumerate(corner_spots):
+            if far != d:
+                continue
+            spread_rows = jnp.stack(
+                [
+                    jnp.broadcast_to(
+                        corner_g[e, side, which, n * nq + q : n * nq + q + 1, :], (cz, lanes)
+                    )
+                    for q in range(nq)
+                ]
+            )
+            if z_tiles == 2:
+                at = jnp.where(narrow == 0, r - 1, cz - r)
+            else:
+                at = cz - r if which == 0 else r - 1
+            tile = jnp.where(row == at, spread_rows, tile)
+        return tile
+
+    def extended(e, planes):
+        result = {}
+        for x in range(cx):
+            others = [deep_gz[e, t, x].reshape(shape) for t in range(z_tiles - 1)]
+            result[x] = tiles_from(planes[x], others)
+        for side in range(2):
+            for d in range(1, DEPTH + 1):
+                own = deep_gx[e, side, DEPTH - d if side == 0 else d - 1].reshape(shape)
+                others = [corner_tile(e, side, t, d) for t in range(z_tiles - 1)]
+                result[-d if side == 0 else cx - 1 + d] = tiles_from(own, others)
+        return result
+
+    def along_y(p):
+        last = p.ndim - 1
+        lane = lax.broadcasted_iota(jnp.int32, p.shape, last)
+        up, down = pltpu.roll(p, lanes - 1, last), pltpu.roll(p, 1, last)
+        if p.ndim == 4:
+            zero = jnp.zeros_like(p[:, :1])
+            next_up = jnp.concatenate([up[:, 1:], zero], axis=1)
+            next_down = jnp.concatenate([zero, down[:, :-1]], axis=1)
+        else:
+            zero = jnp.zeros_like(p[:1])
+            next_up = jnp.concatenate([up[1:], zero], axis=0)
+            next_down = jnp.concatenate([zero, down[:-1]], axis=0)
+        return jnp.where(lane == lanes - 1, next_up, up), jnp.where(lane == 0, next_down, down)
+
+    def along_z(p):
+        at = lax.broadcasted_iota(jnp.int32, p.shape, 2)
+        up, down = pltpu.roll(p, cz - 1, 2), pltpu.roll(p, 1, 2)
+        zero = jnp.zeros_like(p[:1])
+        next_up = jnp.concatenate([up[1:], zero], axis=0)
+        next_down = jnp.concatenate([zero, down[:-1]], axis=0)
+        return jnp.where(at == cz - 1, next_up, up), jnp.where(at == 0, next_down, down)
+
+    for side, x in ((0, 0), (1, cx - 1)):
+        near_x[side, 0] = own_flux[0][x].reshape(plane, lanes)
+        near_x[side, 1] = own_void[x].reshape(plane, lanes)
+    for x in range(cx):
+        near_z[0, x] = own_flux[1][x].reshape(plane, lanes)
+        near_z[1, x] = own_void[x].reshape(plane, lanes)
+    each((0, 1, 2, 3), near_copy, "start")
+    store_deep(0, own_void)
+    each((0, 1, 4, 5, 6, 7), lambda i: deep_copy(0, i), "start")
+
+    void_y = [along_y(v) for v in own_void]
+    flux_y = [along_y(v) for v in own_flux[2]]
+    each((0, 1, 2, 3), near_copy, "wait_recv", True)
+
+    def with_ghosts(planes, field):
+        low = near_gx[0, field].reshape(shape)
+        high = near_gx[1, field].reshape(shape)
+        return [low] + planes + [high]
+
+    flux_x, void_x = with_ghosts(own_flux[0], 0), with_ghosts(own_void, 1)
+    void_inner, pressure = [], []
+    for x in range(cx):
+        flux_z, void_z = [
+            tiles_from(own[x], [near_gz[t, field, x].reshape(shape) for t in range(z_tiles - 1)])
+            for field, own in ((0, own_flux[1]), (1, own_void))
+        ]
+        void_inner.append(void_z)
+        flux_up, flux_down = [own_of(v) for v in along_z(flux_z)]
+        void_up, void_down = [own_of(v) for v in along_z(void_z)]
+        source = -0.5 * (
+            flux_x[x + 2] - flux_x[x] + flux_up - flux_down + flux_y[x][0] - flux_y[x][1]
+        )
+        around = void_x[x + 2] + void_x[x] + void_up + void_down + void_y[x][0] + void_y[x][1]
+        pressure.append(source / (0.5 * (6.0 * own_void[x] + around)))
+
+    def start_pressure(e, planes):
+        store_deep(e, planes)
+        each(range(8), lambda i: deep_copy(e, i), "start")
+
+    def wait_pressure(e, planes):
+        each(range(8), lambda i: deep_copy(e, i), "wait_recv", True)
+        return extended(e, planes)
+
+    start_pressure(1, pressure)
     give_back([growth], sent_growth, 0)
     start_all(2, sent_growth, got_growth)
 
-    source = -0.5 * (
-        beside[0][0] - beside[0][1] + beside[1][2] - beside[1][3] + beside[2][4] - beside[2][5]
-    )
-    here_void = stacked[3]
-    weights = [0.5 * (here_void + beside[3][i]) for i in range(6)]
-    diagonal = weights[0] + weights[1] + weights[2] + weights[3] + weights[4] + weights[5]
-    inverse = 1.0 / diagonal
-    weights = [w * inverse for w in weights]
-    source = source * inverse
-    pressure = source
-    for sweep in range(SWEEPS):
-        around = sides_of(
-            1 + sweep,
-            press.at[sweep],
-            press_z.at[sweep],
-            press_gx.at[sweep],
-            press_gz.at[sweep],
-            [pressure],
-        )[0]
-        if sweep < SWEEPS - 1:
-            total = source
-            for i in range(6):
-                total = total + weights[i] * around[i]
-            pressure = total
-    steps = [around[0] - around[1], around[2] - around[3], around[4] - around[5]]
-    following = [provisional[a] - 0.5 * steps[a].reshape(tiles, lanes) for a in range(3)]
+    each((0, 1, 4, 5, 6, 7), lambda i: deep_copy(0, i), "wait_recv", True)
+    shares = {x: void_inner[x] for x in range(cx)}
+    for side in range(2):
+        for d in range(1, DEPTH + 1):
+            own = deep_gx[0, side, DEPTH - d if side == 0 else d - 1].reshape(shape)
+            others = [corner_tile(0, side, t, d) for t in range(z_tiles - 1)]
+            shares[-d if side == 0 else cx - 1 + d] = tiles_from(own, others)
+    weights = {}
+    for x in range(1 - DEPTH, cx + DEPTH - 1):
+        here = shares[x]
+        nearby = (shares[x + 1], shares[x - 1]) + along_z(here) + along_y(here)
+        sums = [here + v for v in nearby]
+        total = sums[0] + sums[1] + sums[2] + sums[3] + sums[4] + sums[5]
+        factor = jnp.where(here > 0.0, 1.0 / total, 0.0)
+        weights[x] = [v * factor for v in sums]
+
+    event = 1
+    current = wait_pressure(event, pressure)
+    begun = current
+    radius = DEPTH
+    for sweep in range(SWEEPS - 1):
+        if radius == 0:
+            event += 1
+            pressure = [own_of(current[x]) for x in range(cx)]
+            start_pressure(event, pressure)
+            current = wait_pressure(event, pressure)
+            radius = DEPTH
+        radius -= 1
+        later = {}
+        for x in range(-radius, cx + radius):
+            p, w = current[x], weights[x]
+            z_up, z_down = along_z(p)
+            y_up, y_down = along_y(p)
+            later[x] = (
+                begun[x]
+                + (w[0] * current[x + 1] + w[1] * current[x - 1])
+                + (w[2] * z_up + w[3] * z_down)
+                + (w[4] * y_up + w[5] * y_down)
+            )
+        current = later
+    pressure = [own_of(current[x]) for x in range(cx)]
+    steps = [[], [], []]
+    for x in range(cx):
+        z_up, z_down = along_z(current[x])
+        y_up, y_down = along_y(pressure[x])
+        steps[0].append(own_of(current[x + 1]) - own_of(current[x - 1]))
+        steps[1].append(own_of(z_up) - own_of(z_down))
+        steps[2].append(y_up - y_down)
+    following = [
+        provisional[a] - 0.5 * jnp.concatenate(steps[a], axis=0).reshape(tiles, lanes)
+        for a in range(3)
+    ]
     give_back([growth * v for v in following], sent_next, 0)
     start_all(3, sent_next, got_next)
 
@@ -369,7 +494,7 @@
         for q in range(nq):
             cut = slice(q * lanes, (q + 1) * lanes)
             at = (x * nq + q) * cz
-            pressure_ref[x, :, cut] = pressure[x, q]
+            pressure_ref[x, :, cut] = pressure[x][q]
             for a in range(3):
                 next_ref[a, x, :, cut] = following[a][at : at + cz]
 
@@ -419,15 +544,10 @@
         (3, sent_next, got_next),
     ):
         end_all(phase, source, target)
-
-
-def hand_over(*refs):
-    sources, targets, sems = refs[:3], refs[3:6], refs[6]
-    copies = [pltpu.make_async_copy(sources[i], targets[i], sems.at[i]) for i in range(3)]
-    for copy in copies:
-        copy.start()
-    for copy in copies:
-        copy.wait()
+    each((0, 1, 2, 3), near_copy, "wait_send")
+    each((0, 1, 4, 5, 6, 7), lambda i: deep_copy(0, i), "wait_send")
+    for e in range(1, event + 1):
+        each(range(8), lambda i: deep_copy(e, i), "wait_send")
 
 
 def solution(mesh):
@@ -441,7 +561,7 @@
         nq = ny // lanes
         plane = nq * cz
         vmem = pltpu.VMEM
-        any_spec = pl.BlockSpec(memory_space=pl.ANY)
+        hbm_spec = pl.BlockSpec(memory_space=pl.ANY)
         vmem_spec = pl.BlockSpec(memory_space=pltpu.VMEM)
         flux = [
             vmem((n_wide, cap, lanes), f32),
@@ -453,15 +573,19 @@
             vmem((n_wide, 3, cap, lanes), f32),
             vmem((n_wide, 3, cap, lanes), f32),
         ]
+        events = 2 + (SWEEPS - 1) // DEPTH
+        others = 1 if n_narrow == 2 else 2
+        corner_rows = (DEPTH * (DEPTH - 1) // 2 * nq + 7) // 8 * 8
         halo = [
-            vmem((cx, 4 * plane, lanes), f32),
-            vmem((2, 4 * cx * nq, lanes), f32),
-            vmem((2, 4 * plane, lanes), f32),
-            vmem((2, 4 * cx * nq, lanes), f32),
-            vmem((SWEEPS, cx, plane, lanes), f32),
-            vmem((SWEEPS, 2, cx * nq, lanes), f32),
-            vmem((SWEEPS, 2, plane, lanes), f32),
-            vmem((SWEEPS, 2, cx * nq, lanes), f32),
+            vmem((2, 2, plane, lanes), f32),
+            vmem((2, 2, plane, lanes), f32),
+            vmem((2, cx, plane, lanes), f32),
+            vmem((others, 2, cx, plane, lanes), f32),
+            vmem((events, cx, plane, lanes), f32),
+            vmem((events, 2, DEPTH, plane, lanes), f32),
+            vmem((events, others, cx, plane, lanes), f32),
+            vmem((events, 2, 2, corner_rows, lanes), f32),
+            vmem((events, 2, others, corner_rows, lanes), f32),
         ]
         drag, pressure, following = pl.pallas_call(
             functools.partial(body, n_wide, n_narrow, cap),
@@ -470,7 +594,7 @@
                 jax.ShapeDtypeStruct((cx, cz, ny), f32),
                 jax.ShapeDtypeStruct((3, cx, cz, ny), f32),
             ),
-            in_specs=[any_spec] * 6,
+            in_specs=[hbm_spec] * 6,
             out_specs=(vmem_spec,) * 3,
             scratch_shapes=[
                 vmem((blocks, particles, lanes), f32),
@@ -488,8 +612,8 @@
                 pltpu.SemaphoreType.DMA((6,)),
                 pltpu.SemaphoreType.DMA((4, n_wide)),
                 pltpu.SemaphoreType.DMA((4, n_wide)),
-                pltpu.SemaphoreType.DMA((SWEEPS + 1, 4)),
-                pltpu.SemaphoreType.DMA((SWEEPS + 1, 4)),
+                pltpu.SemaphoreType.DMA((events + 1, 8)),
+                pltpu.SemaphoreType.DMA((events + 1, 8)),
             ],
             compiler_params=pltpu.CompilerParams(
                 collective_id=0, has_side_effects=True, vmem_limit_bytes=60 * 1024 * 1024
@@ -502,14 +626,6 @@
             block_tile.reshape(1, blocks),
             fluid_velocity,
         )
-        results = (drag, pressure, following)
-        drag, pressure, following = pl.pallas_call(
-            hand_over,
-            out_shape=tuple(jax.ShapeDtypeStruct(r.shape, r.dtype) for r in results),
-            in_specs=[any_spec] * 3,
-            out_specs=(any_spec,) * 3,
-            scratch_shapes=[pltpu.SemaphoreType.DMA((3,))],
-        )(*results)
         return jnp.transpose(drag, (1, 0, 2)), pressure, following
 
     return jax.shard_map(

time: 65.6 us -> 46.7 us (0.71)
  Pallas kernels: 64.8 us -> 41.2 us
  local copies, waits for them, and re-layouts: 0 us -> 4.63 us
    pallas_call x1 -> x0, Pallas kernels: 12 us -> none  [local(): pl.pallas_call(hand_over, out_shape=tuple((jax.ShapeDtypeStruct(r.shape,...]
    pallas_call x1, Pallas kernels: 52.8 us -> 41.2 us  [local(): pl.pallas_call(functools.partial(body, n_wide, n_narrow, cap), out_shape=...]
    unnamed x0 -> x3, local copies, waits for them, and re-layouts: none -> 4.63 us
where the time goes in v3:
time: 46.7 us; the launch traced here: 46.4 us
  Pallas kernels  41.2 us (88%)
  local copies, waits for them, and re-layouts  4.63 us (10%)
  between operations  0.64 us (1%)
    pallas_call x1, Pallas kernels, local(): pl.pallas_call(functools.partial(body, n_wide, n_narrow, cap), out_shape=...  41.2 us
    unnamed x3, local copies, waits for them, and re-layouts  4.63 us

profile of v3, /device:TPU:0, one launch (start us, length us, event | category | flops | bytes accessed | tf_op | source)
XLA Modules:
  0.0 46.4 jit_solution(7273341004161925295)
XLA Ops:
  0.6 41.2 %shard_map.85 = (f32[3,64,64]{2,1,0:T(8,128)}, f32[4,8,512]{2,1,0:T(8,128)}, f32[3,4,8,512]{3,2,1,0:T(8,128)}) custom-call(f32[64,64,128]{2,1,0:T(8,128)} %kernel_hbm.1, f32[64,64]{1,0:T(8,128)} %volume_hbm.1, f32[3,64,64]{2,1,0:T(8,128)} %bitcast.4, s32[1,64]{1,0:T(1,128)} %bitcast.6, s32[1,64]{1,0:T(1,128)} %bitcast.7, f32[3,4,8,512]{3,2,1,0:T(8,128)} %fluid_hbm.1), custom_call_target="tpu_custom_call" | custom-call | tf_op jit(solution)/shard_map/pallas_call | solution.py:590
  41.8 1.5 %copy.12 = f32[64,3,64]{2,0,1:T(8,128)} copy(f32[64,3,64]{2,0,1:T(8,128)} %bitcast.5) | data formatting | bytes 98304
  43.3 1.5 %copy.13 = f32[4,8,512]{2,1,0:T(8,128)} copy(f32[4,8,512]{2,1,0:T(8,128)} %get-tuple-element.13) | data formatting | bytes 131072
  44.8 1.6 %copy.14 = f32[3,4,8,512]{3,2,1,0:T(8,128)} copy(f32[3,4,8,512]{3,2,1,0:T(8,128)} %get-tuple-element.14) | data formatting | bytes 393216

commit v4 on v3

--- a/solution.py
+++ b/solution.py
@@ -125,12 +125,12 @@
     placed_col = target_col * cap + position_col
     slot_col = lax.broadcasted_iota(jnp.int32, (slots, blocks), 0).astype(f32)
     place = jnp.where(slot_col == placed_row, 1.0, 0.0)
-    tile_col = jnp.sum(place * tile_ref[...].astype(f32), axis=1, keepdims=True)
-    sent_tiles[...] = jnp.broadcast_to(tile_col, (slots, lanes)).reshape(n_wide, cap, lanes)
-
-    beside_x = jnp.where(wide > 0, 1, 0) + jnp.where(wide < n_wide - 1, 1, 0)
-    beside_z = jnp.where(narrow > 0, 1, 0) + jnp.where(narrow < n_narrow - 1, 1, 0)
-    pl.semaphore_wait(barrier, n_wide - 1 + beside_z * (1 + beside_x))
+    named = lax.broadcasted_iota(jnp.int32, (n_wide, blocks), 0).astype(f32) == target_row[:1]
+    named = jnp.where(named, tile_ref[...].astype(f32), 0.0)
+    at_lane = lax.broadcasted_iota(jnp.int32, (blocks, lanes), 1).astype(f32) == position_col
+    at_lane = jnp.where(at_lane, 1.0, 0.0).astype(bf16)
+    high, low = split(named)
+    sent_tiles[...] = (dot(high, at_lane) + dot(low, at_lane)).reshape(n_wide, 1, lanes)
 
     def passing(phase, source, target, step):
         partner = lax.rem(wide + step, n_wide)
@@ -144,11 +144,13 @@
         )
 
     def start_all(phase, source, target):
-        def go(step, carry):
+        def go(turn, carry):
+            far = (turn + 1) // 2
+            step = n_wide // 2 + far * (2 * (turn % 2) - 1)
             passing(phase, source, target, step).start()
             return carry
 
-        lax.fori_loop(1, n_wide, go, 0)
+        lax.fori_loop(0, n_wide - 1, go, 0)
         target[wide] = source[wide]
 
     def wait_all(phase, source, target):
@@ -164,8 +166,6 @@
             return carry
 
         lax.fori_loop(1, n_wide, go, 0)
-
-    start_all(0, sent_tiles, got_tiles)
 
     loads[2].wait()
     loads[3].wait()
@@ -200,6 +200,11 @@
         split(rows[pl.ds(k, blocks, stride=8), :] + rows[pl.ds(4 + k, blocks, stride=8), :])
         for k in range(4)
     ]
+    beside_x = jnp.where(wide > 0, 1, 0) + jnp.where(wide < n_wide - 1, 1, 0)
+    beside_z = jnp.where(narrow > 0, 1, 0) + jnp.where(narrow < n_narrow - 1, 1, 0)
+    pl.semaphore_wait(barrier, n_wide - 1 + beside_z * (1 + beside_x))
+
+    start_all(0, sent_tiles, got_tiles)
     right = jnp.concatenate(
         [jnp.concatenate([o[0] for o in own], axis=1), jnp.concatenate([o[1] for o in own], axis=1)],
         axis=0,
@@ -214,7 +219,10 @@
     order = lax.broadcasted_iota(jnp.int32, (slots, tiles), 1)
     x_of, q_of, z_of = order // plane, (order // cz) % nq, order % cz
     tile_of = ((x_of * cz + z_of) * nq + q_of).astype(f32)
-    tile_slots = got_tiles[...].reshape(slots, lanes)
+    tile_rows = jnp.broadcast_to(got_tiles[...], (n_wide, cap, lanes)).reshape(slots, lanes)
+    slot_at = lax.broadcasted_iota(jnp.int32, (slots, lanes), 0) % cap
+    lane_at = lax.broadcasted_iota(jnp.int32, (slots, lanes), 1)
+    tile_slots = jnp.sum(jnp.where(slot_at == lane_at, tile_rows, 0.0), axis=1, keepdims=True)
     selector = jnp.where(tile_slots == tile_of, 1.0, 0.0)
     turned = jnp.transpose(selector).astype(bf16)
     selector = selector.astype(bf16)
@@ -433,7 +441,6 @@
 
     start_pressure(1, pressure)
     give_back([growth], sent_growth, 0)
-    start_all(2, sent_growth, got_growth)
 
     each((0, 1, 4, 5, 6, 7), lambda i: deep_copy(0, i), "wait_recv", True)
     shares = {x: void_inner[x] for x in range(cx)}
@@ -453,6 +460,7 @@
 
     event = 1
     current = wait_pressure(event, pressure)
+    start_all(2, sent_growth, got_growth)
     begun = current
     radius = DEPTH
     for sweep in range(SWEEPS - 1):
@@ -561,11 +569,11 @@
         nq = ny // lanes
         plane = nq * cz
         vmem = pltpu.VMEM
-        hbm_spec = pl.BlockSpec(memory_space=pl.ANY)
+        hbm_spec = pl.BlockSpec(memory_space=pltpu.HBM)
         vmem_spec = pl.BlockSpec(memory_space=pltpu.VMEM)
         flux = [
-            vmem((n_wide, cap, lanes), f32),
-            vmem((n_wide, cap, lanes), f32),
+            vmem((n_wide, 1, lanes), f32),
+            vmem((n_wide, 1, lanes), f32),
             vmem((n_wide, 4, cap, lanes), f32),
             vmem((n_wide, 4, cap, lanes), f32),
             vmem((n_wide, 1, cap, lanes), f32),
@@ -616,15 +624,20 @@
                 pltpu.SemaphoreType.DMA((events + 1, 8)),
             ],
             compiler_params=pltpu.CompilerParams(
-                collective_id=0, has_side_effects=True, vmem_limit_bytes=60 * 1024 * 1024
+                collective_id=0, has_side_effects=True, vmem_limit_bytes=40 * 1024 * 1024
             ),
         )(
-            kernel,
-            volume,
-            jnp.transpose(velocity, (1, 0, 2)),
-            block_brick.reshape(1, blocks),
-            block_tile.reshape(1, blocks),
-            fluid_velocity,
+            *[
+                pltpu.with_memory_space_constraint(operand, pltpu.HBM)
+                for operand in (
+                    kernel,
+                    volume,
+                    jnp.transpose(velocity, (1, 0, 2)),
+                    block_brick.reshape(1, blocks),
+                    block_tile.reshape(1, blocks),
+                    fluid_velocity,
+                )
+            ]
         )
         return jnp.transpose(drag, (1, 0, 2)), pressure, following
 

time: 46.7 us -> 44 us (0.942)
  local copies, waits for them, and re-layouts: 4.63 us -> 1.95 us
    unnamed x3, local copies, waits for them, and re-layouts: 4.63 us -> 1.95 us
where the time goes in v4:
time: 44 us; the launch traced here: 43.9 us
  Pallas kernels  41.3 us (94%)
  local copies, waits for them, and re-layouts  1.95 us (4%)
  between operations  0.64 us (1%)
    pallas_call x1, Pallas kernels, local(): pl.pallas_call(functools.partial(body, n_wide, n_narrow, cap), out_shape=...  41.3 us
    unnamed x3, local copies, waits for them, and re-layouts  1.95 us

profile of v4, /device:TPU:0, one launch (start us, length us, event | category | flops | bytes accessed | tf_op | source)
XLA Modules:
  0.0 43.9 jit_solution(8521984327087838843)
XLA Ops:
  0.6 41.3 %shard_map.85 = (f32[3,64,64]{2,1,0:T(8,128)S(1)}, f32[4,8,512]{2,1,0:T(8,128)S(1)}, f32[3,4,8,512]{3,2,1,0:T(8,128)S(1)}) custom-call(f32[64,64,128]{2,1,0:T(8,128)} %kernel_hbm.1, f32[64,64]{1,0:T(8,128)} %volume_hbm.1, f32[3,64,64]{2,1,0:T(8,128)} %bitcast.5, s32[1,64]{1,0:T(1,128)} %bitcast.6, s32[1,64]{1,0:T(1,128)} %bitcast.7, f32[3,4,8,512]{3,2,1,0:T(8,128)} %fluid_hbm.1), custom_call_target="tpu_custom_call" | custom-call | tf_op jit(solution)/shard_map/pallas_call | solution.py:598
  41.9 0.6 %copy.12 = f32[64,3,64]{2,0,1:T(8,128)} copy(f32[64,3,64]{2,0,1:T(8,128)S(1)} %bitcast.4) | data formatting | bytes 98304
  42.6 0.6 %copy.13 = f32[4,8,512]{2,1,0:T(8,128)} copy(f32[4,8,512]{2,1,0:T(8,128)S(1)} %get-tuple-element.13) | data formatting | bytes 131072
  43.2 0.7 %copy.14 = f32[3,4,8,512]{3,2,1,0:T(8,128)} copy(f32[3,4,8,512]{3,2,1,0:T(8,128)S(1)} %get-tuple-element.14) | data formatting | bytes 393216

commit v5 on v4

--- a/solution.py
+++ b/solution.py
@@ -28,7 +28,7 @@
     n_wide, n_narrow, cap,
     kernel_hbm, volume_hbm, velocity_hbm, brick_hbm, tile_hbm, fluid_hbm,
     drag_ref, pressure_ref, next_ref,
-    kernel_buf, volume_ref, velocity_ref, brick_ref, tile_ref, fluid_ref, pieces, rows, sent_tiles, got_tiles, sent, got,
+    kernel_buf, volume_ref, velocity_ref, brick_ref, tile_ref, fluid_ref, pieces, turned_pieces, rows, products, sent_tiles, got_tiles, sent, got,
     sent_growth, got_growth, sent_next, got_next,
     near_x, near_gx, near_z, near_gz, deep, deep_gx, deep_gz, corner, corner_g,
     load_sem, send_sem, recv_sem, side_send, side_recv,
@@ -179,25 +179,15 @@
             [low, jnp.zeros_like(low)], axis=1
         )
     loads[4].wait()
-    group = 8
-
-    def contract(step, carry):
-        base = pl.multiple_of(step * group, group)
-        weights = kernel_buf[pl.ds(base, group)]
-        high, low = split(weights)
-        both = jnp.concatenate([high, low], axis=1)
-        pieces[pl.ds(base, group)] = both
-        at = pl.ds(pl.multiple_of(base * 8, 8), group * 8)
-        left = rows[at, :].reshape(group, 8, lanes).astype(bf16)
-        out = lax.dot_general(
-            left, both, (((2,), (1,)), ((0,), (0,))), preferred_element_type=f32
-        )
-        rows[at, :] = out.reshape(group * 8, lanes)
-        return carry
-
-    lax.fori_loop(0, blocks // group, contract, 0)
+    for b in range(blocks):
+        both = jnp.concatenate(split(kernel_buf[b]), axis=0)
+        pieces[b] = both
+        at = slice(b * 8, b * 8 + 8)
+        products[at, :] = dot(rows[at, :].astype(bf16), both)
     own = [
-        split(rows[pl.ds(k, blocks, stride=8), :] + rows[pl.ds(4 + k, blocks, stride=8), :])
+        split(
+            products[pl.ds(k, blocks, stride=8), :] + products[pl.ds(4 + k, blocks, stride=8), :]
+        )
         for k in range(4)
     ]
     beside_x = jnp.where(wide > 0, 1, 0) + jnp.where(wide < n_wide - 1, 1, 0)
@@ -214,6 +204,15 @@
     for k in range(4):
         sent[:, k] = in_slots[:, k * lanes : (k + 1) * lanes].reshape(n_wide, cap, lanes)
     start_all(1, sent, got)
+
+    group = 8
+
+    def turn(step, carry):
+        for b in range(group):
+            turned_pieces[step * group + b] = jnp.transpose(pieces[step * group + b])
+        return carry
+
+    lax.fori_loop(0, blocks // group, turn, 0)
 
     wait_all(0, sent_tiles, got_tiles)
     order = lax.broadcasted_iota(jnp.int32, (slots, tiles), 1)
@@ -521,24 +520,13 @@
     for k in range(3):
         place_back(got_next, k, k)
 
-    def sample(step, carry):
-        base = pl.multiple_of(step * group, group)
-        at = pl.ds(pl.multiple_of(base * 8, 8), group * 8)
-        left = rows[at, :].reshape(group, 8, lanes).astype(bf16)
-        out = lax.dot_general(
-            left,
-            pieces[pl.ds(base, group)],
-            (((2,), (2,)), ((0,), (0,))),
-            preferred_element_type=f32,
-        )
-        rows[at, :] = out.reshape(group * 8, lanes)
-        return carry
-
-    lax.fori_loop(0, blocks // group, sample, 0)
+    for b in range(blocks):
+        at = slice(b * 8, b * 8 + 8)
+        products[at, :] = dot(rows[at, :].astype(bf16), turned_pieces[b])
 
     def sampled(k):
-        top = rows[pl.ds(k, blocks, stride=8), :]
-        low = rows[pl.ds(4 + k, blocks, stride=8), :]
+        top = products[pl.ds(k, blocks, stride=8), :]
+        low = products[pl.ds(4 + k, blocks, stride=8), :]
         return (top + low)[:, :particles] + pltpu.roll(top, particles, 1)[:, :particles]
 
     fourth = sampled(3)
@@ -556,6 +544,15 @@
     each((0, 1, 4, 5, 6, 7), lambda i: deep_copy(0, i), "wait_send")
     for e in range(1, event + 1):
         each(range(8), lambda i: deep_copy(e, i), "wait_send")
+
+
+def hand_over(*refs):
+    sources, targets, sems = refs[:3], refs[3:6], refs[6]
+    copies = [pltpu.make_async_copy(sources[i], targets[i], sems.at[i]) for i in range(3)]
+    for copy in copies:
+        copy.start()
+    for copy in copies:
+        copy.wait()
 
 
 def solution(mesh):
@@ -612,6 +609,8 @@
                 vmem((1, blocks), jnp.int32),
                 vmem((3, cx, cz, ny), f32),
                 vmem((blocks, 2 * particles, lanes), bf16),
+                vmem((blocks, lanes, 2 * particles), bf16),
+                vmem((blocks * 8, lanes), f32),
                 vmem((blocks * 8, lanes), f32),
             ]
             + flux
@@ -639,6 +638,15 @@
                 )
             ]
         )
+        results = (drag, pressure, following)
+        drag, pressure, following = pl.pallas_call(
+            hand_over,
+            out_shape=tuple(jax.ShapeDtypeStruct(r.shape, r.dtype) for r in results),
+            in_specs=[vmem_spec] * 3,
+            out_specs=(pl.BlockSpec(memory_space=pltpu.HBM),) * 3,
+            scratch_shapes=[pltpu.SemaphoreType.DMA((3,))],
+            compiler_params=pltpu.CompilerParams(vmem_limit_bytes=4 * 1024 * 1024),
+        )(*results)
         return jnp.transpose(drag, (1, 0, 2)), pressure, following
 
     return jax.shard_map(

time: 44 us -> 40.8 us (0.927)
  local copies, waits for them, and re-layouts: 1.95 us -> 0 us
  Pallas kernels: 41.3 us -> 40 us
    pallas_call x1, Pallas kernels: 41.3 us -> 39.3 us  [local(): pl.pallas_call(functools.partial(body, n_wide, n_narrow, cap), out_shape=...]
    unnamed x3 -> x0, local copies, waits for them, and re-layouts: 1.95 us -> none
    pallas_call x0 -> x1, Pallas kernels: none -> 0.76 us  [local(): pl.pallas_call(hand_over, out_shape=tuple((jax.ShapeDtypeStruct(r.shape,...]
where the time goes in v5:
time: 40.8 us; the launch traced here: 40.7 us
  Pallas kernels  40 us (98%)
  between operations  0.64 us (2%)
    pallas_call x1, Pallas kernels, local(): pl.pallas_call(functools.partial(body, n_wide, n_narrow, cap), out_shape=...  39.3 us

profile of v5, /device:TPU:0, one launch (start us, length us, event | category | flops | bytes accessed | tf_op | source)
XLA Modules:
  0.0 40.7 jit_solution(2154895912360789522)
XLA Ops:
  0.6 39.3 %shard_map.85 = (f32[3,64,64]{2,1,0:T(8,128)S(1)}, f32[4,8,512]{2,1,0:T(8,128)S(1)}, f32[3,4,8,512]{3,2,1,0:T(8,128)S(1)}) custom-call(f32[64,64,128]{2,1,0:T(8,128)} %kernel_hbm.1, f32[64,64]{1,0:T(8,128)} %volume_hbm.1, f32[3,64,64]{2,1,0:T(8,128)} %bitcast.4, s32[1,64]{1,0:T(1,128)} %bitcast.5, s32[1,64]{1,0:T(1,128)} %bitcast.6, f32[3,4,8,512]{3,2,1,0:T(8,128)} %fluid_hbm.1), custom_call_target="tpu_custom_call" | custom-call | tf_op jit(solution)/shard_map/pallas_call | solution.py:595
  39.9 0.8 %shard_map.86 = (f32[3,64,64]{2,1,0:T(8,128)}, f32[4,8,512]{2,1,0:T(8,128)}, f32[3,4,8,512]{3,2,1,0:T(8,128)}) custom-call(f32[3,64,64]{2,1,0:T(8,128)S(1)} %get-tuple-element.9.refs_0_, f32[4,8,512]{2,1,0:T(8,128)S(1)} %get-tuple-element.10.refs_1_, f32[3,4,8,512]{3,2,1,0:T(8,128)S(1)} %get-tuple-element.11.refs_2_), custom_call_target="tpu_custom_call" | custom-call | tf_op jit(solution)/shard_map/pallas_call | solution.py:642

commit v6 on v5

--- a/solution.py
+++ b/solution.py
@@ -9,6 +9,7 @@
 
 SWEEPS = 6
 DEPTH = 3
+LOAD_PARTS = 4
 DIRECTIONS = ((-1, 0), (1, 0), (0, -1), (0, 1), (-1, -1), (-1, 1), (1, -1), (1, 1))
 MESH = pl.DeviceIdType.MESH
 f32 = jnp.float32
@@ -49,12 +50,19 @@
                 (tile_hbm, tile_ref),
                 (volume_hbm, volume_ref),
                 (velocity_hbm, velocity_ref),
-                (kernel_hbm, kernel_buf),
                 (fluid_hbm, fluid_ref),
             )
         )
     ]
-    for load in loads:
+    part = blocks // LOAD_PARTS
+    for i in range(LOAD_PARTS):
+        rows_of = pl.ds(i * part, part)
+        loads.append(
+            pltpu.make_async_copy(
+                kernel_hbm.at[rows_of], kernel_buf.at[rows_of], load_sem.at[5 + i]
+            )
+        )
+    for load in loads[:4] + loads[5:] + loads[4:5]:
         load.start()
 
     barrier = pltpu.get_barrier_semaphore()
@@ -137,8 +145,8 @@
         return pltpu.make_async_remote_copy(
             src_ref=source.at[partner],
             dst_ref=target.at[wide],
-            send_sem=send_sem.at[phase, step],
-            recv_sem=recv_sem.at[phase, step],
+            send_sem=send_sem.at[phase],
+            recv_sem=recv_sem.at[phase],
             device_id=(partner, narrow),
             device_id_type=MESH,
         )
@@ -153,19 +161,22 @@
         lax.fori_loop(0, n_wide - 1, go, 0)
         target[wide] = source[wide]
 
+    def whole(phase, source, target):
+        others = pl.ds(0, n_wide - 1)
+        return pltpu.make_async_remote_copy(
+            src_ref=source.at[others],
+            dst_ref=target.at[others],
+            send_sem=send_sem.at[phase],
+            recv_sem=recv_sem.at[phase],
+            device_id=(lax.rem(wide + 1, n_wide), narrow),
+            device_id_type=MESH,
+        )
+
     def wait_all(phase, source, target):
-        def go(step, carry):
-            passing(phase, source, target, step).wait_recv()
-            return carry
-
-        lax.fori_loop(1, n_wide, go, 0)
+        whole(phase, source, target).wait_recv()
 
     def end_all(phase, source, target):
-        def go(step, carry):
-            passing(phase, source, target, step).wait_send()
-            return carry
-
-        lax.fori_loop(1, n_wide, go, 0)
+        whole(phase, source, target).wait_send()
 
     loads[2].wait()
     loads[3].wait()
@@ -178,8 +189,9 @@
         rows[pl.ds(4 + k, blocks, stride=8), :] = jnp.concatenate(
             [low, jnp.zeros_like(low)], axis=1
         )
-    loads[4].wait()
     for b in range(blocks):
+        if b % part == 0:
+            loads[5 + b // part].wait()
         both = jnp.concatenate(split(kernel_buf[b]), axis=0)
         pieces[b] = both
         at = slice(b * 8, b * 8 + 8)
@@ -228,7 +240,7 @@
     turned = jnp.concatenate([turned, turned], axis=1)
     selector = jnp.concatenate([selector, selector], axis=1)
 
-    loads[5].wait()
+    loads[4].wait()
     fluid = [
         jnp.concatenate(
             [
@@ -440,6 +452,9 @@
 
     start_pressure(1, pressure)
     give_back([growth], sent_growth, 0)
+    end_all(0, sent_tiles, got_tiles)
+    end_all(1, sent, got)
+    each((0, 1, 2, 3), near_copy, "wait_send")
 
     each((0, 1, 4, 5, 6, 7), lambda i: deep_copy(0, i), "wait_recv", True)
     shares = {x: void_inner[x] for x in range(cx)}
@@ -514,6 +529,10 @@
         rows[pl.ds(row, blocks, stride=8), :] = out[:, :lanes]
         rows[pl.ds(4 + row, blocks, stride=8), :] = out[:, lanes:]
 
+    end_all(2, sent_growth, got_growth)
+    each((0, 1, 4, 5, 6, 7), lambda i: deep_copy(0, i), "wait_send")
+    for e in range(1, event + 1):
+        each(range(8), lambda i: deep_copy(e, i), "wait_send")
     wait_all(2, sent_growth, got_growth)
     place_back(got_growth, 0, 3)
     wait_all(3, sent_next, got_next)
@@ -533,17 +552,7 @@
     for k in range(3):
         drag_ref[k] = volume * sampled(k) - carried[1 + k] * fourth
 
-    for phase, source, target in (
-        (0, sent_tiles, got_tiles),
-        (1, sent, got),
-        (2, sent_growth, got_growth),
-        (3, sent_next, got_next),
-    ):
-        end_all(phase, source, target)
-    each((0, 1, 2, 3), near_copy, "wait_send")
-    each((0, 1, 4, 5, 6, 7), lambda i: deep_copy(0, i), "wait_send")
-    for e in range(1, event + 1):
-        each(range(8), lambda i: deep_copy(e, i), "wait_send")
+    end_all(3, sent_next, got_next)
 
 
 def hand_over(*refs):
@@ -616,9 +625,9 @@
             + flux
             + halo
             + [
-                pltpu.SemaphoreType.DMA((6,)),
-                pltpu.SemaphoreType.DMA((4, n_wide)),
-                pltpu.SemaphoreType.DMA((4, n_wide)),
+                pltpu.SemaphoreType.DMA((5 + LOAD_PARTS,)),
+                pltpu.SemaphoreType.DMA((4,)),
+                pltpu.SemaphoreType.DMA((4,)),
                 pltpu.SemaphoreType.DMA((events + 1, 8)),
                 pltpu.SemaphoreType.DMA((events + 1, 8)),
             ],

time: 40.8 us -> 39.1 us (0.958)
  Pallas kernels: 40 us -> 38.3 us
    pallas_call x1, Pallas kernels: 39.3 us -> 37.5 us  [local(): pl.pallas_call(functools.partial(body, n_wide, n_narrow, cap), out_shape=...]
where the time goes in v6:
time: 39.1 us; the launch traced here: 38.9 us
  Pallas kernels  38.3 us (98%)
  between operations  0.64 us (2%)
    pallas_call x1, Pallas kernels, local(): pl.pallas_call(functools.partial(body, n_wide, n_narrow, cap), out_shape=...  37.5 us

profile of v6, /device:TPU:0, one launch (start us, length us, event | category | flops | bytes accessed | tf_op | source)
XLA Modules:
  0.0 38.9 jit_solution(4667688196713068095)
XLA Ops:
  0.6 37.5 %shard_map.85 = (f32[3,64,64]{2,1,0:T(8,128)S(1)}, f32[4,8,512]{2,1,0:T(8,128)S(1)}, f32[3,4,8,512]{3,2,1,0:T(8,128)S(1)}) custom-call(f32[64,64,128]{2,1,0:T(8,128)} %kernel_hbm.1, f32[64,64]{1,0:T(8,128)} %volume_hbm.1, f32[3,64,64]{2,1,0:T(8,128)} %bitcast.4, s32[1,64]{1,0:T(1,128)} %bitcast.5, s32[1,64]{1,0:T(1,128)} %bitcast.6, f32[3,4,8,512]{3,2,1,0:T(8,128)} %fluid_hbm.1), custom_call_target="tpu_custom_call" | custom-call | tf_op jit(solution)/shard_map/pallas_call | solution.py:604
  38.2 0.8 %shard_map.86 = (f32[3,64,64]{2,1,0:T(8,128)}, f32[4,8,512]{2,1,0:T(8,128)}, f32[3,4,8,512]{3,2,1,0:T(8,128)}) custom-call(f32[3,64,64]{2,1,0:T(8,128)S(1)} %get-tuple-element.9.refs_0_, f32[4,8,512]{2,1,0:T(8,128)S(1)} %get-tuple-element.10.refs_1_, f32[3,4,8,512]{3,2,1,0:T(8,128)S(1)} %get-tuple-element.11.refs_2_), custom_call_target="tpu_custom_call" | custom-call | tf_op jit(solution)/shard_map/pallas_call | solution.py:651

commit v7 on v6

--- a/solution.py
+++ b/solution.py
@@ -152,13 +152,10 @@
         )
 
     def start_all(phase, source, target):
-        def go(turn, carry):
+        for turn in range(n_wide - 1):
             far = (turn + 1) // 2
             step = n_wide // 2 + far * (2 * (turn % 2) - 1)
             passing(phase, source, target, step).start()
-            return carry
-
-        lax.fori_loop(0, n_wide - 1, go, 0)
         target[wide] = source[wide]
 
     def whole(phase, source, target):
@@ -330,15 +327,17 @@
 
     corner_spots = [(d, r) for d in range(1, DEPTH) for r in range(1, DEPTH + 1 - d)]
 
-    def store_deep(e, planes):
+    def send_deep(e, planes, directions):
         for x in range(cx):
             deep[e, x] = planes[x].reshape(plane, lanes)
+        each(directions, lambda i: deep_copy(e, i), "start")
         for sx in range(2):
             for sz in range(2):
                 for n, (d, r) in enumerate(corner_spots):
                     x = d - 1 if sx == 0 else cx - d
                     z = r - 1 if sz == 0 else cz - r
                     corner[e, sx, sz, n * nq : (n + 1) * nq, :] = planes[x][:, z, :]
+        each((4, 5, 6, 7), lambda i: deep_copy(e, i), "start")
 
     row = lax.broadcasted_iota(jnp.int32, shape, 1)
 
@@ -410,12 +409,15 @@
     for side, x in ((0, 0), (1, cx - 1)):
         near_x[side, 0] = own_flux[0][x].reshape(plane, lanes)
         near_x[side, 1] = own_void[x].reshape(plane, lanes)
+    each((0, 1), near_copy, "start")
     for x in range(cx):
         near_z[0, x] = own_flux[1][x].reshape(plane, lanes)
         near_z[1, x] = own_void[x].reshape(plane, lanes)
-    each((0, 1, 2, 3), near_copy, "start")
-    store_deep(0, own_void)
-    each((0, 1, 4, 5, 6, 7), lambda i: deep_copy(0, i), "start")
+    each((2, 3), near_copy, "start")
+    send_deep(0, own_void, (0, 1))
+
+    give_back([growth], sent_growth, 0)
+    start_all(2, sent_growth, got_growth)
 
     void_y = [along_y(v) for v in own_void]
     flux_y = [along_y(v) for v in own_flux[2]]
@@ -443,15 +445,13 @@
         pressure.append(source / (0.5 * (6.0 * own_void[x] + around)))
 
     def start_pressure(e, planes):
-        store_deep(e, planes)
-        each(range(8), lambda i: deep_copy(e, i), "start")
+        send_deep(e, planes, (0, 1, 2, 3))
 
     def wait_pressure(e, planes):
         each(range(8), lambda i: deep_copy(e, i), "wait_recv", True)
         return extended(e, planes)
 
     start_pressure(1, pressure)
-    give_back([growth], sent_growth, 0)
     end_all(0, sent_tiles, got_tiles)
     end_all(1, sent, got)
     each((0, 1, 2, 3), near_copy, "wait_send")
@@ -474,7 +474,6 @@
 
     event = 1
     current = wait_pressure(event, pressure)
-    start_all(2, sent_growth, got_growth)
     begun = current
     radius = DEPTH
     for sweep in range(SWEEPS - 1):

time: 39.1 us -> 38.7 us (0.990)
  Pallas kernels: 38.3 us -> 37.9 us
    pallas_call x1, Pallas kernels: 37.5 us -> 37.1 us  [local(): pl.pallas_call(functools.partial(body, n_wide, n_narrow, cap), out_shape=...]
where the time goes in v7:
time: 38.7 us; the launch traced here: 38.5 us
  Pallas kernels  37.9 us (98%)
  between operations  0.64 us (2%)
    pallas_call x1, Pallas kernels, local(): pl.pallas_call(functools.partial(body, n_wide, n_narrow, cap), out_shape=...  37.1 us

profile of v7, /device:TPU:0, one launch (start us, length us, event | category | flops | bytes accessed | tf_op | source)
XLA Modules:
  0.0 38.5 jit_solution(13226379547062794939)
XLA Ops:
  0.6 37.1 %shard_map.85 = (f32[3,64,64]{2,1,0:T(8,128)S(1)}, f32[4,8,512]{2,1,0:T(8,128)S(1)}, f32[3,4,8,512]{3,2,1,0:T(8,128)S(1)}) custom-call(f32[64,64,128]{2,1,0:T(8,128)} %kernel_hbm.1, f32[64,64]{1,0:T(8,128)} %volume_hbm.1, f32[3,64,64]{2,1,0:T(8,128)} %bitcast.4, s32[1,64]{1,0:T(1,128)} %bitcast.5, s32[1,64]{1,0:T(1,128)} %bitcast.6, f32[3,4,8,512]{3,2,1,0:T(8,128)} %fluid_hbm.1), custom_call_target="tpu_custom_call" | custom-call | tf_op jit(solution)/shard_map/pallas_call | solution.py:603
  37.7 0.8 %shard_map.86 = (f32[3,64,64]{2,1,0:T(8,128)}, f32[4,8,512]{2,1,0:T(8,128)}, f32[3,4,8,512]{3,2,1,0:T(8,128)}) custom-call(f32[3,64,64]{2,1,0:T(8,128)S(1)} %get-tuple-element.9.refs_0_, f32[4,8,512]{2,1,0:T(8,128)S(1)} %get-tuple-element.10.refs_1_, f32[3,4,8,512]{3,2,1,0:T(8,128)S(1)} %get-tuple-element.11.refs_2_), custom_call_target="tpu_custom_call" | custom-call | tf_op jit(solution)/shard_map/pallas_call | solution.py:650

commit v8 on v7

--- a/solution.py
+++ b/solution.py
@@ -199,11 +199,6 @@
         )
         for k in range(4)
     ]
-    beside_x = jnp.where(wide > 0, 1, 0) + jnp.where(wide < n_wide - 1, 1, 0)
-    beside_z = jnp.where(narrow > 0, 1, 0) + jnp.where(narrow < n_narrow - 1, 1, 0)
-    pl.semaphore_wait(barrier, n_wide - 1 + beside_z * (1 + beside_x))
-
-    start_all(0, sent_tiles, got_tiles)
     right = jnp.concatenate(
         [jnp.concatenate([o[0] for o in own], axis=1), jnp.concatenate([o[1] for o in own], axis=1)],
         axis=0,
@@ -212,7 +207,12 @@
     in_slots = dot(place, right)
     for k in range(4):
         sent[:, k] = in_slots[:, k * lanes : (k + 1) * lanes].reshape(n_wide, cap, lanes)
+    beside_x = jnp.where(wide > 0, 1, 0) + jnp.where(wide < n_wide - 1, 1, 0)
+    beside_z = jnp.where(narrow > 0, 1, 0) + jnp.where(narrow < n_narrow - 1, 1, 0)
+    pl.semaphore_wait(barrier, n_wide - 1 + beside_z * (1 + beside_x))
+
     start_all(1, sent, got)
+    start_all(0, sent_tiles, got_tiles)
 
     group = 8
 
@@ -221,7 +221,8 @@
             turned_pieces[step * group + b] = jnp.transpose(pieces[step * group + b])
         return carry
 
-    lax.fori_loop(0, blocks // group, turn, 0)
+    turned_first = blocks // group * 3 // 4
+    lax.fori_loop(0, turned_first, turn, 0)
 
     wait_all(0, sent_tiles, got_tiles)
     order = lax.broadcasted_iota(jnp.int32, (slots, tiles), 1)
@@ -481,6 +482,8 @@
             event += 1
             pressure = [own_of(current[x]) for x in range(cx)]
             start_pressure(event, pressure)
+            if event == 2:
+                lax.fori_loop(turned_first, blocks // group, turn, 0)
             current = wait_pressure(event, pressure)
             radius = DEPTH
         radius -= 1
@@ -522,21 +525,22 @@
     slot_row = lax.broadcasted_iota(jnp.int32, (blocks, slots), 1).astype(f32)
     back = jnp.where(slot_row == placed_col, 1.0, 0.0).astype(bf16)
 
-    def place_back(target, k, row):
-        high, low = split(target[:, k].reshape(slots, lanes))
-        out = dot(back, jnp.concatenate([high, low], axis=1))
-        rows[pl.ds(row, blocks, stride=8), :] = out[:, :lanes]
-        rows[pl.ds(4 + row, blocks, stride=8), :] = out[:, lanes:]
+    def place_back(target, found):
+        parts = [split(target[:, k].reshape(slots, lanes)) for k in range(len(found))]
+        out = dot(back, jnp.concatenate([half for pair in parts for half in pair], axis=1))
+        for k, row in enumerate(found):
+            for half in range(2):
+                cut = slice((2 * k + half) * lanes, (2 * k + half + 1) * lanes)
+                rows[pl.ds(4 * half + row, blocks, stride=8), :] = out[:, cut]
 
     end_all(2, sent_growth, got_growth)
     each((0, 1, 4, 5, 6, 7), lambda i: deep_copy(0, i), "wait_send")
     for e in range(1, event + 1):
         each(range(8), lambda i: deep_copy(e, i), "wait_send")
     wait_all(2, sent_growth, got_growth)
-    place_back(got_growth, 0, 3)
+    place_back(got_growth, (3,))
     wait_all(3, sent_next, got_next)
-    for k in range(3):
-        place_back(got_next, k, k)
+    place_back(got_next, (0, 1, 2))
 
     for b in range(blocks):
         at = slice(b * 8, b * 8 + 8)

time: 38.7 us -> 39.9 us (1.031)
  Pallas kernels: 37.9 us -> 39.1 us
    pallas_call x1, Pallas kernels: 37.1 us -> 38.3 us  [local(): pl.pallas_call(functools.partial(body, n_wide, n_narrow, cap), out_shape=...]
where the time goes in v8:
time: 39.9 us; the launch traced here: 39.7 us
  Pallas kernels  39.1 us (98%)
  between operations  0.64 us (2%)
    pallas_call x1, Pallas kernels, local(): pl.pallas_call(functools.partial(body, n_wide, n_narrow, cap), out_shape=...  38.3 us

profile of v8, /device:TPU:0, one launch (start us, length us, event | category | flops | bytes accessed | tf_op | source)
XLA Modules:
  0.0 39.7 jit_solution(13176247317682613942)
XLA Ops:
  0.6 38.3 %shard_map.85 = (f32[3,64,64]{2,1,0:T(8,128)S(1)}, f32[4,8,512]{2,1,0:T(8,128)S(1)}, f32[3,4,8,512]{3,2,1,0:T(8,128)S(1)}) custom-call(f32[64,64,128]{2,1,0:T(8,128)} %kernel_hbm.1, f32[64,64]{1,0:T(8,128)} %volume_hbm.1, f32[3,64,64]{2,1,0:T(8,128)} %bitcast.4, s32[1,64]{1,0:T(1,128)} %bitcast.5, s32[1,64]{1,0:T(1,128)} %bitcast.6, f32[3,4,8,512]{3,2,1,0:T(8,128)} %fluid_hbm.1), custom_call_target="tpu_custom_call" | custom-call | tf_op jit(solution)/shard_map/pallas_call | solution.py:607
  38.9 0.8 %shard_map.86 = (f32[3,64,64]{2,1,0:T(8,128)}, f32[4,8,512]{2,1,0:T(8,128)}, f32[3,4,8,512]{3,2,1,0:T(8,128)}) custom-call(f32[3,64,64]{2,1,0:T(8,128)S(1)} %get-tuple-element.9.refs_0_, f32[4,8,512]{2,1,0:T(8,128)S(1)} %get-tuple-element.10.refs_1_, f32[3,4,8,512]{3,2,1,0:T(8,128)S(1)} %get-tuple-element.11.refs_2_), custom_call_target="tpu_custom_call" | custom-call | tf_op jit(solution)/shard_map/pallas_call | solution.py:654
